TPU v7x, 256 devices: a whole 4x4x8 slice. The times are simulated.
256 devices in a mesh: dp: 32 (over x, y, core), ctx: 8 (over z).
Axes of the slice: x: 4, y: 4, z: 8, core: 2. Of those that a mesh axis runs over, the one named last changes fastest.
Arguments:
- queries: bfloat16 [32768, 2048], P(('dp', 'ctx')), may hold values from -5 to 5
- keys: bfloat16 [32768, 2048], P(('dp', 'ctx')), may hold values from -5 to 5
- values: bfloat16 [32768, 2048], P(('dp', 'ctx')), may hold values from -6 to 6
- grad_out: bfloat16 [32768, 2048], P(('dp', 'ctx')), may hold values from -6 to 6
- doc_ids: int32 [32768], replicated, may hold values from 0 to 32512, as said below
- tile_pairs: int32 [768, 2], replicated, may hold values from -1 to 255, as said below
Outputs:
- attended: bfloat16 [32768, 2048], P(('dp', 'ctx'))
- grad_q: bfloat16 [32768, 2048], P(('dp', 'ctx'))
- grad_k: bfloat16 [32768, 2048], P(('dp', 'ctx'))
- grad_v: bfloat16 [32768, 2048], P(('dp', 'ctx'))
Inputs may be any that keep to these rules, and one draw needn't show every extreme that they name: `doc_ids`: documents lie end to end, so ids never fall; no document holds more than 256 tokens; all but the batch's last two hold 64 to 256 tokens, some exactly 256; the last document begins at token 32512. `tile_pairs`: each used row holds an owner tile and a partner tile no lower than it; the used rows are exactly the pairs of tiles that hold tokens of one common document, each pair once, in no particular order; the other rows hold -1 in both columns.
All inputs are finite; a program needn't handle non-finite values.
Results may differ from a plain program's by a relative error of at most 0.029.
Values may be sent and summed in bfloat16 or wider, within the bound.
A program may use at most 128 MiB of HBM per device.

v0:
```python
import math

import jax
import jax.numpy as jnp
from jax import lax
from jax.sharding import PartitionSpec as P

HEAD = 128
TILE = 128


def passed_along(block, axis, distance):
    devices = range(lax.axis_size(axis))
    route = [(i - distance, i) for i in devices if i - distance in devices]
    return lax.ppermute(block, axis, route)


def listed(pairs, first_tiles, second_tiles):
    owner = pairs[:, 0][:, None, None]
    partner = pairs[:, 1][:, None, None]
    first = first_tiles[None, :, None]
    second = second_tiles[None, None, :]
    found = (owner == first) & (partner == second) | (owner == second) & (partner == first)
    return jnp.any(found, axis=0)


def token_mask(pairs, first_ids, second_ids, first_start, second_start, first_count, second_count):
    first_tiles = first_start // TILE + jnp.arange(first_count // TILE, dtype=jnp.int32)
    second_tiles = second_start // TILE + jnp.arange(second_count // TILE, dtype=jnp.int32)
    tiled = listed(pairs, first_tiles, second_tiles)
    spread = jnp.repeat(jnp.repeat(tiled, TILE, axis=0), TILE, axis=1)
    return spread & (first_ids[:, None] == second_ids[None, :])


def masked_scores(left, right, mask, scale):
    scores = jnp.einsum("agd,bgd->gab", left, right, preferred_element_type=jnp.float32) * scale
    return jnp.where(mask[None], scores, -jnp.inf)


def body(queries, keys, values, grad_out, doc_ids, tile_pairs):
    rows, width = queries.shape
    reach = 2 * rows
    window = rows + 2 * reach
    head = HEAD
    heads = width // head
    per_pass = min(4, heads)
    scale = 1.0 / math.sqrt(head)
    index = lax.axis_index(("dp", "ctx"))
    filler = -jnp.ones((reach,), jnp.int32)
    padded_ids = jnp.concatenate([filler, doc_ids, filler])
    start = index * rows
    own_ids = lax.dynamic_slice_in_dim(doc_ids, start, rows, 0)
    near_ids = lax.dynamic_slice_in_dim(padded_ids, start, window, 0)
    forward_mask = token_mask(tile_pairs, own_ids, near_ids, start, start - reach, rows, window)
    both = jnp.concatenate([keys, values], axis=1)
    moved = {}
    for hop in (2, 1, -1, -2):
        moved[hop] = passed_along(both, ("dp", "ctx"), hop)
    near = jnp.concatenate([moved[2], moved[1], both, moved[-1], moved[-2]], axis=0)
    near_keys = near[:, :width]
    near_values = near[:, width:]
    attended_parts, grad_q_parts, lse_parts, delta_parts = ([], [], [], [])
    key_parts, value_parts = ([], [])
    for group in range(heads // per_pass):
        low_col = group * per_pass * head
        high_col = low_col + per_pass * head
        query = queries[:, low_col:high_col].reshape(rows, per_pass, head)
        grads = grad_out[:, low_col:high_col].reshape(rows, per_pass, head)
        keys_near = near_keys[:, low_col:high_col].reshape(window, per_pass, head)
        values_near = near_values[:, low_col:high_col].reshape(window, per_pass, head)
        scores = masked_scores(query, keys_near, forward_mask, scale)
        top = jnp.max(scores, axis=2, keepdims=True)
        lse = top[:, :, 0] + jnp.log(jnp.sum(jnp.exp(scores - top), axis=2))
        probs = jnp.exp(scores - lse[:, :, None])
        probs_low = probs.astype(jnp.bfloat16)
        attended = jnp.einsum(
            "gab,bgd->agd", probs_low, values_near, preferred_element_type=jnp.float32
        ).astype(jnp.bfloat16)
        delta = jnp.sum(grads.astype(jnp.float32) * attended.astype(jnp.float32), axis=2).T
        dprobs = jnp.einsum("agd,bgd->gab", grads, values_near, preferred_element_type=jnp.float32)
        dscores = (probs * (dprobs - delta[:, :, None])).astype(jnp.bfloat16)
        grad_q = (
            jnp.einsum("gab,bgd->agd", dscores, keys_near, preferred_element_type=jnp.float32)
            * scale
        ).astype(jnp.bfloat16)
        attended_parts.append(attended.reshape(rows, per_pass * head))
        grad_q_parts.append(grad_q.reshape(rows, per_pass * head))
        lse_parts.append(lse)
        delta_parts.append(delta)
        grad_k = (
            jnp.einsum("gab,agd->bgd", dscores, query, preferred_element_type=jnp.float32) * scale
        )
        grad_v = jnp.einsum("gab,agd->bgd", probs_low, grads, preferred_element_type=jnp.float32)
        key_parts.append(grad_k.reshape(window, per_pass * head))
        value_parts.append(grad_v.reshape(window, per_pass * head))
    attended = jnp.concatenate(attended_parts, axis=1)
    grad_q = jnp.concatenate(grad_q_parts, axis=1)
    terms = jnp.concatenate(
        [jnp.concatenate(key_parts, axis=1), jnp.concatenate(value_parts, axis=1)], axis=1
    )
    total = terms[2 * rows : 3 * rows]
    for slot in (0, 1, 3, 4):
        total = total + passed_along(
            terms[slot * rows : (slot + 1) * rows].astype(jnp.bfloat16), ("dp", "ctx"), slot - 2
        ).astype(jnp.float32)
    grad_k = total[:, :width].astype(jnp.bfloat16)
    grad_v = total[:, width:].astype(jnp.bfloat16)
    return (attended, grad_q, grad_k, grad_v)


def solution(mesh):
    in_specs = (
        P(("dp", "ctx"), None),
        P(("dp", "ctx"), None),
        P(("dp", "ctx"), None),
        P(("dp", "ctx"), None),
        P(),
        P(),
    )
    out_specs = (
        P(("dp", "ctx"), None),
        P(("dp", "ctx"), None),
        P(("dp", "ctx"), None),
        P(("dp", "ctx"), None),
    )
    return jax.shard_map(body, mesh=mesh, in_specs=in_specs, out_specs=out_specs, check_vma=False)
```

profile of v0, /device:TPU:0, one launch (start us, length us, event | category | flops | bytes accessed | tf_op | source)
XLA Modules:
  0.0 225.8 jit_solution(14996385007485474904)
XLA Ops:
  0.6 1.4 copy.127
  2.3 1.1 pad_maximum_fusion
  3.4 4.4 %collective-permute-start = (bf16[128,4096]{0,1:T(8,128)(2,1)}, bf16[128,4096]{0,1:T(8,128)(2,1)}, u32[]{:S(2)}, u32[]{:S(2)}) collective-permute-start(bf16[128,4096]{0,1:T(8,128)(2,1)} %pad_maximum_fusion), channel_id=1, source_target_pairs={{0,2},{1,3},{2,4},{3,5},{4,6},{5,7},{6,8},{7,9},{8,10},{9,11},{10,... | collective-permute-start | bytes 3145736 | tf_op jit(solution)/shard_map/ppermute | solution.py:15
  7.8 4.8 %collective-permute-start.1 = (bf16[128,4096]{0,1:T(8,128)(2,1)}, bf16[128,4096]{0,1:T(8,128)(2,1)}, u32[]{:S(2)}, u32[]{:S(2)}) collective-permute-start(bf16[128,4096]{0,1:T(8,128)(2,1)} %pad_maximum_fusion), channel_id=1, source_target_pairs={{0,1},{1,2},{2,3},{3,4},{4,5},{5,6},{6,7},{7,8},{8,9},{9,10},{10,1... | collective-permute-start | bytes 3145736 | tf_op jit(solution)/shard_map/ppermute | solution.py:15
  12.6 1.3 collective-permute-start.2
  13.9 1.3 collective-permute-start.3
  17.2 22.4 %collective-permute-done = bf16[128,4096]{0,1:T(8,128)(2,1)} collective-permute-done((bf16[128,4096]{0,1:T(8,128)(2,1)}, bf16[128,4096]{0,1:T(8,128)(2,1)}, u32[]{:S(2)}, u32[]{:S(2)}) %collective-permute-start) | collective-permute-done | bytes 1048608 | tf_op jit(solution)/shard_map/ppermute | solution.py:15
  39.6 1.4 constant_dynamic-update-slice_fusion.4
  41.0 33.6 %collective-permute-done.1 = bf16[128,4096]{0,1:T(8,128)(2,1)} collective-permute-done((bf16[128,4096]{0,1:T(8,128)(2,1)}, bf16[128,4096]{0,1:T(8,128)(2,1)}, u32[]{:S(2)}, u32[]{:S(2)}) %collective-permute-start.1) | collective-permute-done | bytes 1048608 | tf_op jit(solution)/shard_map/ppermute | solution.py:15
  74.6 1.5 constant_dynamic-update-slice_fusion.3
  76.3 1.5 constant_dynamic-update-slice_fusion.1
  77.8 6.9 %collective-permute-done.3 = bf16[128,4096]{0,1:T(8,128)(2,1)} collective-permute-done((bf16[128,4096]{0,1:T(8,128)(2,1)}, bf16[128,4096]{0,1:T(8,128)(2,1)}, u32[]{:S(2)}, u32[]{:S(2)}) %collective-permute-start.3) | collective-permute-done | bytes 1048608 | tf_op jit(solution)/shard_map/ppermute | solution.py:15
  84.7 1.5 constant_dynamic-update-slice_fusion
  86.2 0.5 fusion.51
  87.3 1.0 multiply_reduce_fusion
  88.8 1.0 fusion.35
  89.8 1.4 fusion.4
  91.2 1.5 fusion.36
  94.6 1.0 multiply_reduce_fusion.1
  95.6 1.5 fusion.39
  97.1 1.3 fusion.25
  98.4 1.0 multiply_reduce_fusion.2
  99.4 1.5 fusion.42
  101.3 1.0 multiply_reduce_fusion.3
  102.3 1.4 fusion.45
  104.7 1.4 fusion.7
  106.1 2.8 %copy.170 = f32[640,4,128]{0,2,1:T(8,128)} copy(f32[640,4,128]{2,0,1:T(8,128)} %fusion.7) | data formatting | bytes 2621440 | tf_op jit(solution)/shard_map/mul | solution.py:91
  108.9 2.5 %constant_dynamic-update-slice_fusion.12 = f32[640,4096]{0,1:T(8,128)} fusion(f32[640,512]{0,1:T(8,128)} %bitcast.181), kind=kLoop, calls=%fused_computation.92 | loop fusion | bytes 2621440
  111.4 1.4 fusion.6
  112.8 2.8 %copy.173 = f32[640,4,128]{0,2,1:T(8,128)} copy(f32[640,4,128]{2,0,1:T(8,128)} %fusion.6) | data formatting | bytes 2621440 | tf_op jit(solution)/shard_map/mul | solution.py:91
  115.6 2.5 %fusion.5 = f32[640,4,128]{2,0,1:T(8,128)} fusion(bf16[4,128,640]{1,2,0:T(8,128)(2,1)} %fusion.25, bf16[128,4,128]{0,2,1:T(8,128)(2,1)S(1)} %bitcast.191), kind=kOutput, calls=%fused_computation.8 | convolution fusion | flops 84213760 | bytes 2097152 | tf_op jit(solution)/shard_map/gab,agd->bgd/dot_general | solution.py:91
  118.1 3.0 %copy.176 = f32[640,4,128]{0,2,1:T(8,128)} copy(f32[640,4,128]{2,0,1:T(8,128)} %fusion.5) | data formatting | bytes 2621440 | tf_op jit(solution)/shard_map/mul | solution.py:91
  121.0 2.8 %copy.179 = f32[640,4,128]{0,2,1:T(8,128)} copy(f32[640,4,128]{2,0,1:T(8,128)} %fusion.4) | data formatting | bytes 2621440 | tf_op jit(solution)/shard_map/mul | solution.py:91
  123.8 2.6 %constant_dynamic-update-slice_fusion.11 = f32[640,4096]{0,1:T(8,128)} fusion(f32[640,4096]{0,1:T(8,128)} %constant_dynamic-update-slice_fusion.12, f32[640,512]{0,1:T(8,128)} %bitcast.178), kind=kLoop, calls=%fused_computation.91 | loop fusion | bytes 2621440
  126.4 1.2 constant_dynamic-update-slice_fusion.10
  127.6 0.6 copy-done.5
  128.2 1.2 constant_dynamic-update-slice_fusion.9
  129.4 0.6 copy-done.4
  130.0 1.2 constant_dynamic-update-slice_fusion.8
  131.2 0.6 copy-done.3
  131.8 1.1 constant_dynamic-update-slice_fusion.7
  132.9 0.6 copy-done.2
  133.6 1.2 constant_dynamic-update-slice_fusion.6
  134.8 0.5 copy-done.1
  135.3 1.1 constant_dynamic-update-slice_fusion.5
  136.5 4.5 %convert.10 = bf16[640,4096]{0,1:T(8,128)(2,1)S(1)} convert(f32[640,4096]{0,1:T(8,128)} %constant_dynamic-update-slice_fusion.5) | non-fusion elementwise | flops 2621440 | bytes 15728640 | tf_op jit(solution)/shard_map/convert.5
  141.0 2.4 %fusion.50 = (bf16[128,4096]{0,1:T(8,128)(2,1)}, bf16[128,4096]{0,1:T(8,128)(2,1)}, bf16[128,4096]{0,1:T(8,128)(2,1)}, bf16[128,4096]{0,1:T(8,128)(2,1)}) fusion(bf16[640,4096]{0,1:T(8,128)(2,1)S(1)} %convert.10), kind=kLoop, calls=%fused_computation.106 | loop fusion | bytes 8388608 | tf_op jit(solution)/shard_map/slice | solution.py:104
  143.4 5.7 %collective-permute-start.7 = (bf16[128,4096]{0,1:T(8,128)(2,1)}, bf16[128,4096]{0,1:T(8,128)(2,1)}, u32[]{:S(2)}, u32[]{:S(2)}) collective-permute-start(bf16[128,4096]{0,1:T(8,128)(2,1)} %get-tuple-element.15), channel_id=1, source_target_pairs={{0,2},{1,3},{2,4},{3,5},{4,6},{5,7},{6,8},{7,9},{8,10},{9,11},{10,... | collective-permute-start | bytes 3145736 | tf_op jit(solution)/shard_map/ppermute | solution.py:15
  149.2 2.8 %collective-permute-start.6 = (bf16[128,4096]{0,1:T(8,128)(2,1)}, bf16[128,4096]{0,1:T(8,128)(2,1)}, u32[]{:S(2)}, u32[]{:S(2)}) collective-permute-start(bf16[128,4096]{0,1:T(8,128)(2,1)} %get-tuple-element.16), channel_id=1, source_target_pairs={{0,1},{1,2},{2,3},{3,4},{4,5},{5,6},{6,7},{7,8},{8,9},{9,10},{10,1... | collective-permute-start | bytes 3145736 | tf_op jit(solution)/shard_map/ppermute | solution.py:15
  151.9 1.3 collective-permute-start.5
  153.2 1.3 collective-permute-start.4
  154.5 1.0 fusion.34
  155.8 1.0 copy.145
  156.8 1.0 copy.144
  157.8 1.0 copy.167
  158.8 1.0 copy.166
  160.7 0.8 pad_maximum_fusion.1
  161.6 0.8 pad_maximum_fusion.2
  162.4 25.8 %collective-permute-done.7 = bf16[128,4096]{0,1:T(8,128)(2,1)} collective-permute-done((bf16[128,4096]{0,1:T(8,128)(2,1)}, bf16[128,4096]{0,1:T(8,128)(2,1)}, u32[]{:S(2)}, u32[]{:S(2)}) %collective-permute-start.7) | collective-permute-done | bytes 1048608 | tf_op jit(solution)/shard_map/ppermute | solution.py:15
  188.2 22.9 %collective-permute-done.6 = bf16[128,4096]{0,1:T(8,128)(2,1)} collective-permute-done((bf16[128,4096]{0,1:T(8,128)(2,1)}, bf16[128,4096]{0,1:T(8,128)(2,1)}, u32[]{:S(2)}, u32[]{:S(2)}) %collective-permute-start.6) | collective-permute-done | bytes 1048608 | tf_op jit(solution)/shard_map/ppermute | solution.py:15
  211.1 9.2 %collective-permute-done.4 = bf16[128,4096]{0,1:T(8,128)(2,1)} collective-permute-done((bf16[128,4096]{0,1:T(8,128)(2,1)}, bf16[128,4096]{0,1:T(8,128)(2,1)}, u32[]{:S(2)}, u32[]{:S(2)}) %collective-permute-start.4) | collective-permute-done | bytes 1048608 | tf_op jit(solution)/shard_map/ppermute | solution.py:15
  220.3 3.4 %fusion.3 = bf16[128,4096]{0,1:T(8,128)(2,1)S(1)} fusion(f32[640,4096]{0,1:T(8,128)} %constant_dynamic-update-slice_fusion.5, bf16[128,4096]{0,1:T(8,128)(2,1)} %collective-permute-done.7, bf16[128,4096]{0,1:T(8,128)(2,1)} %collective-permute-done.6, bf16[128,4096]{0,1:T(8,128)(2,1)} %collective-permute-done.5, bf16[128,4096]{0,1:T(8,128)(2,1)} %collective-permute-done.4), kind=kLoop, calls=%fused_computation.4 | loop fusion | flops 4718592 | bytes 7340032 | tf_op jit(solution)/shard_map/convert.1
  223.8 1.0 copy.184
  224.8 1.0 copy.185
  (76 shorter events, 7.8 us)
Async XLA Ops:
  0.6 1.4 copy-start.13
  2.3 12.9 %copy-start.14 = (bf16[128,2048]{1,0:T(8,128)(2,1)S(1)}, bf16[128,2048]{1,0:T(8,128)(2,1)}, u32[]{:S(2)}) copy-start(bf16[128,2048]{1,0:T(8,128)(2,1)} %param.9) | copy-start | bytes 1572868
  2.3 13.0 %copy-start.17 = (s32[768,2]{0,1:T(2,128)S(1)}, s32[768,2]{0,1:T(2,128)}, u32[]{:S(2)}) copy-start(s32[768,2]{0,1:T(2,128)} %param.11) | copy-start | bytes 18436
  2.3 13.1 %copy-start.16 = (s32[32768]{0:T(1024)S(1)}, s32[32768]{0:T(1024)}, u32[]{:S(2)}) copy-start(s32[32768]{0:T(1024)} %param.10) | copy-start | bytes 393220
  2.3 13.2 %copy-start.15 = (bf16[128,2048]{1,0:T(8,128)(2,1)S(1)}, bf16[128,2048]{1,0:T(8,128)(2,1)}, u32[]{:S(2)}) copy-start(bf16[128,2048]{1,0:T(8,128)(2,1)} %param.6) | copy-start | bytes 1572868
  3.4 36.2 %collective-permute-start = (bf16[128,4096]{0,1:T(8,128)(2,1)}, bf16[128,4096]{0,1:T(8,128)(2,1)}, u32[]{:S(2)}, u32[]{:S(2)}) collective-permute-start(bf16[128,4096]{0,1:T(8,128)(2,1)} %pad_maximum_fusion), channel_id=1, source_target_pairs={{0,2},{1,3},{2,4},{3,5},{4,6},{5,7},{6,8},{7,9},{8,10},{9,11},{10,... | collective-permute-start | bytes 3145736 | tf_op jit(solution)/shard_map/ppermute | solution.py:15
  7.8 66.8 %collective-permute-start.1 = (bf16[128,4096]{0,1:T(8,128)(2,1)}, bf16[128,4096]{0,1:T(8,128)(2,1)}, u32[]{:S(2)}, u32[]{:S(2)}) collective-permute-start(bf16[128,4096]{0,1:T(8,128)(2,1)} %pad_maximum_fusion), channel_id=1, source_target_pairs={{0,1},{1,2},{2,3},{3,4},{4,5},{5,6},{6,7},{7,8},{8,9},{9,10},{10,1... | collective-permute-start | bytes 3145736 | tf_op jit(solution)/shard_map/ppermute | solution.py:15
  12.6 63.7 %collective-permute-start.2 = (bf16[128,4096]{0,1:T(8,128)(2,1)}, bf16[128,4096]{0,1:T(8,128)(2,1)}, u32[]{:S(2)}, u32[]{:S(2)}) collective-permute-start(bf16[128,4096]{0,1:T(8,128)(2,1)} %pad_maximum_fusion), channel_id=1, source_target_pairs={{1,0},{2,1},{3,2},{4,3},{5,4},{6,5},{7,6},{8,7},{9,8},{10,9},{11,1... | collective-permute-start | bytes 3145736 | tf_op jit(solution)/shard_map/ppermute | solution.py:15
  13.9 70.8 %collective-permute-start.3 = (bf16[128,4096]{0,1:T(8,128)(2,1)}, bf16[128,4096]{0,1:T(8,128)(2,1)}, u32[]{:S(2)}, u32[]{:S(2)}) collective-permute-start(bf16[128,4096]{0,1:T(8,128)(2,1)} %pad_maximum_fusion), channel_id=1, source_target_pairs={{2,0},{3,1},{4,2},{5,3},{6,4},{7,5},{8,6},{9,7},{10,8},{11,9},{12,... | collective-permute-start | bytes 3145736 | tf_op jit(solution)/shard_map/ppermute | solution.py:15
  16.4 76.9 %copy-start.7 = (bf16[128,512]{0,1:T(8,128)(2,1)}, bf16[128,512]{0,1:T(8,128)(2,1)S(1)}, u32[]{:S(2)}) copy-start(bf16[128,512]{0,1:T(8,128)(2,1)S(1)} %copy.223) | copy-start | bytes 393220
  16.7 77.3 %copy-start.9 = (bf16[128,512]{0,1:T(8,128)(2,1)}, bf16[128,512]{0,1:T(8,128)(2,1)S(1)}, u32[]{:S(2)}) copy-start(bf16[128,512]{0,1:T(8,128)(2,1)S(1)} %copy.222) | copy-start | bytes 393220
  103.8 0.9 copy-start.10
  108.9 2.5 %copy-start.8 = (bf16[128,512]{0,1:T(8,128)(2,1)S(1)}, bf16[128,512]{0,1:T(8,128)(2,1)}, u32[]{:S(2)}) copy-start(bf16[128,512]{0,1:T(8,128)(2,1)} %copy-done.7) | copy-start | bytes 393220
  123.8 2.6 %copy-start.6 = (f32[640,4,128]{0,2,1:T(8,128)S(1)}, f32[640,4,128]{0,2,1:T(8,128)}, u32[]{:S(2)}) copy-start(f32[640,4,128]{0,2,1:T(8,128)} %copy.176) | copy-start | bytes 3932164
  126.4 1.8 copy-start.5
  128.2 1.8 copy-start.4
  130.0 1.8 copy-start.3
  131.8 1.8 copy-start.2
  133.5 1.8 copy-start.1
  141.0 13.5 %copy-start = (bf16[4,128,640]{1,2,0:T(8,128)(2,1)S(1)}, bf16[4,128,640]{1,2,0:T(8,128)(2,1)}, u32[]{:S(2)}) copy-start(bf16[4,128,640]{1,2,0:T(8,128)(2,1)} %fusion.25) | copy-start | bytes 1966084
  143.4 12.1 %copy-start.11 = (bf16[4,128,128]{2,1,0:T(8,128)(2,1)S(1)}, bf16[4,128,128]{2,1,0:T(8,128)(2,1)}, u32[]{:S(2)}) copy-start(bf16[4,128,128]{2,1,0:T(8,128)(2,1)} %get-tuple-element.45) | copy-start | bytes 393220
  143.4 12.2 %copy-start.12 = (bf16[4,128,128]{2,1,0:T(8,128)(2,1)S(1)}, bf16[4,128,128]{2,1,0:T(8,128)(2,1)}, u32[]{:S(2)}) copy-start(bf16[4,128,128]{2,1,0:T(8,128)(2,1)} %get-tuple-element.47) | copy-start | bytes 393220
  143.4 44.8 %collective-permute-start.7 = (bf16[128,4096]{0,1:T(8,128)(2,1)}, bf16[128,4096]{0,1:T(8,128)(2,1)}, u32[]{:S(2)}, u32[]{:S(2)}) collective-permute-start(bf16[128,4096]{0,1:T(8,128)(2,1)} %get-tuple-element.15), channel_id=1, source_target_pairs={{0,2},{1,3},{2,4},{3,5},{4,6},{5,7},{6,8},{7,9},{8,10},{9,11},{10,... | collective-permute-start | bytes 3145736 | tf_op jit(solution)/shard_map/ppermute | solution.py:15
  149.2 61.9 %collective-permute-start.6 = (bf16[128,4096]{0,1:T(8,128)(2,1)}, bf16[128,4096]{0,1:T(8,128)(2,1)}, u32[]{:S(2)}, u32[]{:S(2)}) collective-permute-start(bf16[128,4096]{0,1:T(8,128)(2,1)} %get-tuple-element.16), channel_id=1, source_target_pairs={{0,1},{1,2},{2,3},{3,4},{4,5},{5,6},{6,7},{7,8},{8,9},{9,10},{10,1... | collective-permute-start | bytes 3145736 | tf_op jit(solution)/shard_map/ppermute | solution.py:15
  151.9 59.1 %collective-permute-start.5 = (bf16[128,4096]{0,1:T(8,128)(2,1)}, bf16[128,4096]{0,1:T(8,128)(2,1)}, u32[]{:S(2)}, u32[]{:S(2)}) collective-permute-start(bf16[128,4096]{0,1:T(8,128)(2,1)} %get-tuple-element.17), channel_id=1, source_target_pairs={{1,0},{2,1},{3,2},{4,3},{5,4},{6,5},{7,6},{8,7},{9,8},{10,9},{11,1... | collective-permute-start | bytes 3145736 | tf_op jit(solution)/shard_map/ppermute | solution.py:15
  153.2 67.0 %collective-permute-start.4 = (bf16[128,4096]{0,1:T(8,128)(2,1)}, bf16[128,4096]{0,1:T(8,128)(2,1)}, u32[]{:S(2)}, u32[]{:S(2)}) collective-permute-start(bf16[128,4096]{0,1:T(8,128)(2,1)} %get-tuple-element.14), channel_id=1, source_target_pairs={{2,0},{3,1},{4,2},{5,3},{6,4},{7,5},{8,6},{9,7},{10,8},{11,9},{12,... | collective-permute-start | bytes 3145736 | tf_op jit(solution)/shard_map/ppermute | solution.py:15
where the time goes:
time: 229 us; the launch traced here: 226 us
  waiting for transfers between devices  121 us (53%)
  local copies, waits for them, and re-layouts  45.1 us (20%)
  matrix products  23.5 us (10%)
  starting transfers between devices  22.9 us (10%)
  other arithmetic  12.3 us (5%)
    ppermute x8, waiting for transfers between devices, passed_along(): return lax.ppermute(block, axis, route)  121 us
    unnamed x54, local copies, waits for them, and re-layouts  23 us
    ppermute x8, starting transfers between devices, passed_along(): return lax.ppermute(block, axis, route)  22.9 us
    mul x4, local copies, waits for them, and re-layouts, body(): jnp.einsum('gab,agd->bgd', dscores, query, preferred_element_type=jnp.flo...  11.3 us
    another operation x2, other arithmetic  7.95 us
    dot_general x4, matrix products, body(): jnp.einsum('gab,agd->bgd', dscores, query, preferred_element_type=jnp.flo...  6.68 us
    dot_general x4, matrix products, body(): jnp.einsum('gab,agd->bgd', probs_low, grads, preferred_element_type=jnp.f...  5.85 us
  transfers between devices with their start and end apart: 8, of which 6 were waited for; matrix products, arithmetic and copies ran while one was open for 6% of the time, Pallas kernels for 0%

commit v1 on v0

v1 whole, which is shorter than its diff:
```python
import functools
import math

import jax
import jax.numpy as jnp
from jax import lax
from jax.experimental import pallas as pl
from jax.experimental.pallas import tpu as pltpu
from jax.sharding import PartitionSpec as P

HEAD = 128
TILE = 128
HALF = 8
PER = 2
GROUPS = HALF // PER
WIDE = PER * HEAD
SPLIT = HALF * HEAD
SCALE = 1.0 / math.sqrt(HEAD)
LOG2E = math.log2(math.e)
FAR = -1e30
MESH_ID = pl.DeviceIdType.MESH


def dot_nt(a, b):
    return lax.dot_general(a, b, (((1,), (1,)), ((), ())), preferred_element_type=jnp.float32)


def dot_nn(a, b):
    return lax.dot_general(a, b, (((1,), (0,)), ((), ())), preferred_element_type=jnp.float32)


def dot_tn(a, b):
    return lax.dot_general(a, b, (((0,), (0,)), ((), ())), preferred_element_type=jnp.float32)


def columns(start, size):
    return pl.ds(pl.multiple_of(start, HEAD), size)


def kernel(
    n_dp, n_ctx,
    q_ref, k_ref, v_ref, g_ref, ids_ref, pairs_ref,
    att_ref, gq_ref, gk_ref, gv_ref,
    own, near, stage, result, late, done, bias_a, bias_b,
    own_sem, e1_send, e1_recv, e2_send, e2_recv, late_send, late_recv, out_sem,
):
    n = n_dp * n_ctx
    me = lax.axis_index("dp") * n_ctx + lax.axis_index("ctx")
    right = lax.rem(me + 1, n)
    left = lax.rem(me + n - 1, n)
    target = [(x // n_ctx, lax.rem(x, n_ctx)) for x in (right, left)]
    inputs = (q_ref, k_ref, v_ref, g_ref)
    outputs = (att_ref, gq_ref, gk_ref, gv_ref)

    def own_copy(a):
        return pltpu.make_async_copy(inputs[a], own.at[a], own_sem.at[a])

    def first(d, g, a):
        cols = columns(g * WIDE, WIDE)
        return pltpu.make_async_remote_copy(
            src_ref=inputs[a].at[:, cols], dst_ref=near.at[d, a, :, cols],
            send_sem=e1_send.at[d, g, a], recv_sem=e1_recv.at[d, g, a],
            device_id=target[d], device_id_type=MESH_ID,
        )

    def second(d, g):
        return pltpu.make_async_remote_copy(
            src_ref=stage.at[d, :, :, columns(g * WIDE, WIDE)],
            dst_ref=near.at[d, :, :, columns(SPLIT + g * WIDE, WIDE)],
            send_sem=e2_send.at[d, g], recv_sem=e2_recv.at[d, g],
            device_id=target[d], device_id_type=MESH_ID,
        )

    def third(d, g):
        cols = columns(g * WIDE, WIDE)
        return pltpu.make_async_remote_copy(
            src_ref=result.at[d, :, :, cols], dst_ref=late.at[d, :, :, cols],
            send_sem=late_send.at[d, g], recv_sem=late_recv.at[d, g],
            device_id=target[d], device_id_type=MESH_ID,
        )

    def out_copy(a, half, g):
        cols = columns(half * SPLIT + g * WIDE, WIDE)
        return pltpu.make_async_copy(done.at[a, :, cols], outputs[a].at[:, cols], out_sem.at[half, g, a])

    for a in range(4):
        own_copy(a).start()
    barrier = pltpu.get_barrier_semaphore()
    for d in range(2):
        pl.semaphore_signal(barrier, inc=1, device_id=target[d], device_id_type=MESH_ID)
    pl.semaphore_wait(barrier, 2)
    for g in range(GROUPS):
        for d in range(2):
            for a in range(4):
                first(d, g, a).start()

    tiles = [lax.rem(me + n + t, n) for t in range(-2, 3)]
    rows = [ids_ref[pl.ds(t, 1), :].astype(jnp.float32) for t in tiles]
    eye = lax.broadcasted_iota(jnp.int32, (TILE, TILE), 0) == lax.broadcasted_iota(jnp.int32, (TILE, TILE), 1)

    def upright(row):
        return jnp.sum(jnp.where(eye, jnp.broadcast_to(row, (TILE, TILE)), 0.0), axis=1, keepdims=True)

    def middle(t):
        before = rows[t - 1][:, TILE - 1 :]
        head, tail = rows[t][:, :1], rows[t][:, TILE - 1 :]
        after = rows[t + 1][:, :1]
        return (before == head) & (head == tail) & (tail == after)

    mid_left, mid_own, mid_right = middle(1), middle(2), middle(3)
    pair_codes = pairs_ref[:, 0:1] * n + pairs_ref[:, 1:2]

    def is_listed(x, y):
        hit = (pair_codes == tiles[x] * n + tiles[y]) | (pair_codes == tiles[y] * n + tiles[x])
        return jnp.max(jnp.where(hit, 1.0, 0.0), axis=0, keepdims=True) > 0.5

    ids_a = [
        jnp.where(mid_left, rows[0], -1.0), rows[1], rows[2], rows[3], jnp.where(mid_right, rows[4], -2.0),
    ]
    ids_b = [jnp.where(mid_left, -1.0, rows[1]), rows[2], jnp.where(mid_right, -2.0, rows[3])]
    up_a = [upright(r) for r in ids_a]
    up_b = [upright(r) for r in ids_b]
    flags = {}
    for x in range(5):
        for y in range(x, min(x + 3, 5)):
            flags[x, y] = is_listed(x, y)
            flags[y, x] = flags[x, y]
    for x in range(5):
        for y in range(5):
            if (x, y) in flags:
                seen = (up_a[x] == ids_a[y]) & flags[x, y]
                bias_a[x * TILE : (x + 1) * TILE, y * TILE : (y + 1) * TILE] = jnp.where(seen, 0.0, FAR)
    for x in range(3):
        for y in range(3):
            seen = (up_b[x] == ids_b[y]) & flags[x + 1, y + 1]
            bias_b[x * TILE : (x + 1) * TILE, y * TILE : (y + 1) * TILE] = jnp.where(seen, 0.0, FAR)
    own_up = upright(rows[2])
    from_left = (own_up == rows[1][:, TILE - 1 :]) & mid_left
    from_right = (own_up == rows[3][:, :1]) & mid_right

    for a in range(4):
        own_copy(a).wait()

    def pass_on(g, carry):
        src = columns(g * WIDE, WIDE)
        for d in range(2):
            for a in range(4):
                first(d, g, a).wait_recv()
            for a in range(4):
                stage[d, a, :, src] = jnp.where(
                    mid_own, near[d, a, :, src], own[a, :, columns(SPLIT + g * WIDE, WIDE)]
                )
            second(d, g).start()
        return carry

    lax.fori_loop(0, GROUPS, pass_on, 0)

    def softmax_parts(query, grads, keys, values, bias):
        scores = dot_nt(query, keys) * (SCALE * LOG2E) + bias
        top = jnp.max(scores, axis=1, keepdims=True)
        weights = jnp.exp2(scores - top)
        inverse = 1.0 / jnp.sum(weights, axis=1, keepdims=True)
        dprobs = dot_nt(grads, values)
        delta = jnp.sum(weights * dprobs, axis=1, keepdims=True) * inverse
        return weights, inverse, dprobs, delta

    def second_half(col):
        at = columns(SPLIT + col, HEAD)
        q, k, v, g = [
            jnp.concatenate([near[0, a, :, at], own[a, :, at], near[1, a, :, at]], axis=0) for a in range(4)
        ]
        probs, dscores = [], []
        where = ((result, 1), (done, None), (result, 0))

        def put(x, a, value):
            ref, d = where[x]
            if d is None:
                ref[a, :, at] = value.astype(jnp.bfloat16)
            else:
                ref[d, a, :, columns(col, HEAD)] = value.astype(jnp.bfloat16)

        for x in range(3):
            r = slice(x * TILE, (x + 1) * TILE)
            weights, inverse, dprobs, delta = softmax_parts(q[r], g[r], k, v, bias_b[r, :])
            p = weights * inverse
            p_low = p.astype(jnp.bfloat16)
            ds = (p * (dprobs - delta)).astype(jnp.bfloat16)
            put(x, 0, dot_nn(p_low, v))
            put(x, 1, dot_nn(ds, k) * SCALE)
            probs.append(p_low)
            dscores.append(ds)
        grad_k = dot_tn(jnp.concatenate(dscores, axis=0), q) * SCALE
        grad_v = dot_tn(jnp.concatenate(probs, axis=0), g)
        for x in range(3):
            r = slice(x * TILE, (x + 1) * TILE)
            put(x, 2, grad_k[r])
            put(x, 3, grad_v[r])

    def first_half(col):
        at, far = columns(col, HEAD), columns(SPLIT + col, HEAD)
        q, k, v, g = [
            jnp.concatenate(
                [near[0, a, :, far], near[0, a, :, at], own[a, :, at], near[1, a, :, at], near[1, a, :, far]], axis=0
            )
            for a in range(4)
        ]
        probs, dscores = [], []
        for x in range(5):
            lo, hi = max(x - 2, 0) * TILE, min(x + 3, 5) * TILE
            if x == 1:
                hi = 4 * TILE
            if x == 3:
                lo = TILE
            r = slice(x * TILE, (x + 1) * TILE)
            weights, inverse, dprobs, delta = softmax_parts(q[r], g[r], k[lo:hi], v[lo:hi], bias_a[r, lo:hi])
            if x == 2:
                p = weights * inverse
                p_low = p.astype(jnp.bfloat16)
                ds = (p * (dprobs - delta)).astype(jnp.bfloat16)
                done[0, :, at] = dot_nn(p_low, v).astype(jnp.bfloat16)
                done[1, :, at] = (dot_nn(ds, k) * SCALE).astype(jnp.bfloat16)
                probs.append(p_low[:, 2 * TILE : 3 * TILE])
                dscores.append(ds[:, 2 * TILE : 3 * TILE])
            else:
                mine = slice(2 * TILE - lo, 3 * TILE - lo)
                p = weights[:, mine] * inverse
                probs.append(p.astype(jnp.bfloat16))
                dscores.append((p * (dprobs[:, mine] - delta)).astype(jnp.bfloat16))
        done[2, :, at] = (dot_tn(jnp.concatenate(dscores, axis=0), q) * SCALE).astype(jnp.bfloat16)
        done[3, :, at] = dot_tn(jnp.concatenate(probs, axis=0), g).astype(jnp.bfloat16)

    def work(g, carry):
        for d in range(2):
            second(d, g).wait_recv()
        def heads_b(j, c):
            second_half(g * WIDE + j * HEAD)
            return c

        def heads_a(j, c):
            first_half(g * WIDE + j * HEAD)
            return c

        lax.fori_loop(0, PER, heads_b, 0)
        for d in range(2):
            third(d, g).start()
        lax.fori_loop(0, PER, heads_a, 0)
        for a in range(4):
            out_copy(a, 0, g).start()
        return carry

    lax.fori_loop(0, GROUPS, work, 0)

    def finish(g, carry):
        cols = columns(g * WIDE, WIDE)
        at = columns(SPLIT + g * WIDE, WIDE)
        for d in range(2):
            third(d, g).wait_recv()
        for a in range(4):
            mixed = jnp.where(from_left, late[0, a, :, cols], done[a, :, at])
            done[a, :, at] = jnp.where(from_right, late[1, a, :, cols], mixed)
        for a in range(4):
            out_copy(a, 1, g).start()
        return carry

    lax.fori_loop(0, GROUPS, finish, 0)

    def drain(g, carry):
        for d in range(2):
            for a in range(4):
                first(d, g, a).wait_send()
            second(d, g).wait_send()
            third(d, g).wait_send()
        for half in range(2):
            for a in range(4):
                out_copy(a, half, g).wait()
        return carry

    lax.fori_loop(0, GROUPS, drain, 0)


def solution(mesh):
    n_dp, n_ctx = mesh.shape["dp"], mesh.shape["ctx"]
    token_spec = P(("dp", "ctx"), None)

    def body(queries, keys, values, grad_out, doc_ids, tile_pairs):
        shape = jax.ShapeDtypeStruct(queries.shape, jnp.bfloat16)
        width = queries.shape[1]
        any_space = pl.BlockSpec(memory_space=pl.ANY)
        in_vmem = pl.BlockSpec(memory_space=pltpu.VMEM)
        low = jnp.bfloat16
        sem = pltpu.SemaphoreType.DMA
        return pl.pallas_call(
            functools.partial(kernel, n_dp, n_ctx),
            out_shape=(shape,) * 4,
            in_specs=[any_space] * 4 + [in_vmem] * 2,
            out_specs=(any_space,) * 4,
            scratch_shapes=[
                pltpu.VMEM((4, TILE, width), low),
                pltpu.VMEM((2, 4, TILE, width), low),
                pltpu.VMEM((2, 4, TILE, SPLIT), low),
                pltpu.VMEM((2, 4, TILE, SPLIT), low),
                pltpu.VMEM((2, 4, TILE, SPLIT), low),
                pltpu.VMEM((4, TILE, width), low),
                pltpu.VMEM((5 * TILE, 5 * TILE), jnp.float32),
                pltpu.VMEM((3 * TILE, 3 * TILE), jnp.float32),
                sem((4,)),
                sem((2, GROUPS, 4)),
                sem((2, GROUPS, 4)),
                sem((2, GROUPS)),
                sem((2, GROUPS)),
                sem((2, GROUPS)),
                sem((2, GROUPS)),
                sem((2, GROUPS, 4)),
            ],
            compiler_params=pltpu.CompilerParams(
                collective_id=0, has_side_effects=True, vmem_limit_bytes=48 * 1024 * 1024
            ),
        )(queries, keys, values, grad_out, doc_ids.reshape(-1, TILE), tile_pairs)

    return jax.shard_map(
        body,
        mesh=mesh,
        in_specs=(token_spec,) * 4 + (P(), P()),
        out_specs=(token_spec,) * 4,
        check_vma=False,
    )
```

time: 229 us -> 87.3 us (0.38); the launches traced: 226 us -> 87 us
  waiting for transfers between devices: 121 us -> 0 us
  Pallas kernels: 0 us -> 78.1 us
  local copies, waits for them, and re-layouts: 45.1 us -> 8.24 us
  matrix products: 23.5 us -> 0 us
  starting transfers between devices: 22.9 us -> 0 us
  other arithmetic: 12.3 us -> 0 us
    ppermute x8 -> x0, waiting for transfers between devices: 121 us -> none  [passed_along(): return lax.ppermute(block, axis, route)]
    pallas_call x0 -> x1, Pallas kernels: none -> 78.1 us  [body(): pl.pallas_call(functools.partial(kernel, n_dp, n_ctx), out_shape=(shape,)...]
    dot_general x24 -> x0, matrix products: 23.5 us -> none  [the longest x4 6.68 us: body(): jnp.einsum('gab,agd->bgd', dscores, query, preferred_element_type=jnp.flo...]
    ppermute x8 -> x0, starting transfers between devices: 22.9 us -> none  [passed_along(): return lax.ppermute(block, axis, route)]
    unnamed x54 -> x15, local copies, waits for them, and re-layouts: 23 us -> 8.24 us
    mul x4 -> x0, local copies, waits for them, and re-layouts: 11.3 us -> none  [body(): jnp.einsum('gab,agd->bgd', dscores, query, preferred_element_type=jnp.flo...]
    another operation x2 -> x0, other arithmetic: 7.95 us -> none
    reshape x8 -> x0, local copies, waits for them, and re-layouts: 4.48 us -> none  [the longest x4 2.24 us: body(): attended_parts.append(attended.reshape(rows, per_pass * head))]
  transfers between devices with their start and end apart: 8 -> 0, of which waited for: 6 -> 0; matrix products, arithmetic and copies ran while one was open for 6% -> 0% of each run, Pallas kernels for 0% -> 0%
where the time goes in v1:
time: 87.3 us; the launch traced here: 87 us
  Pallas kernels  78.1 us (89%)
  local copies, waits for them, and re-layouts  8.24 us (9%)
    pallas_call x1, Pallas kernels, body(): pl.pallas_call(functools.partial(kernel, n_dp, n_ctx), out_shape=(shape,)...  78.1 us
    unnamed x15, local copies, waits for them, and re-layouts  8.24 us

profile of v1, /device:TPU:0, one launch (start us, length us, event | category | flops | bytes accessed | tf_op | source)
XLA Modules:
  0.0 87.0 jit_solution(828761939551235047)
XLA Ops:
  0.6 0.0 copy-start.4
  0.6 0.9 %copy.10.pairs_ref = s32[768,2]{1,0:T(8,128)S(1)} copy(s32[768,2]{0,1:T(2,128)} %param.11) | data formatting | bytes 12288 | tf_op args[5]
  1.6 0.0 copy-done.4
  1.6 0.0 copy-start
  1.6 1.0 %copy-done = bf16[128,2048]{1,0:T(8,128)(2,1)S(1)} copy-done((bf16[128,2048]{1,0:T(8,128)(2,1)S(1)}, bf16[128,2048]{1,0:T(8,128)(2,1)}, u32[]{:S(2)}) %copy-start) | copy-done | bytes 524312
  2.6 0.0 copy-start.1
  2.6 1.0 %copy-done.1 = bf16[128,2048]{1,0:T(8,128)(2,1)S(1)} copy-done((bf16[128,2048]{1,0:T(8,128)(2,1)S(1)}, bf16[128,2048]{1,0:T(8,128)(2,1)}, u32[]{:S(2)}) %copy-start.1) | copy-done | bytes 524312
  3.6 0.0 copy-start.2
  3.6 1.0 %copy-done.2 = bf16[128,2048]{1,0:T(8,128)(2,1)S(1)} copy-done((bf16[128,2048]{1,0:T(8,128)(2,1)S(1)}, bf16[128,2048]{1,0:T(8,128)(2,1)}, u32[]{:S(2)}) %copy-start.2) | copy-done | bytes 524312
  4.7 0.0 copy-start.3
  4.7 1.0 %copy-done.3 = bf16[128,2048]{1,0:T(8,128)(2,1)S(1)} copy-done((bf16[128,2048]{1,0:T(8,128)(2,1)S(1)}, bf16[128,2048]{1,0:T(8,128)(2,1)}, u32[]{:S(2)}) %copy-start.3) | copy-done | bytes 524312
  5.7 78.1 %shard_map.93 = (bf16[128,2048]{1,0:T(8,128)(2,1)S(1)}, bf16[128,2048]{1,0:T(8,128)(2,1)S(1)}, bf16[128,2048]{1,0:T(8,128)(2,1)S(1)}, bf16[128,2048]{1,0:T(8,128)(2,1)S(1)}) custom-call(bf16[128,2048]{1,0:T(8,128)(2,1)S(1)} %copy-done, bf16[128,2048]{1,0:T(8,128)(2,1)S(1)} %copy-done.1, bf16[128,2048]{1,0:T(8,128)(2,1)S(1)} %copy-done.2, ...), custom_call_target="tpu_custom_call" | custom-call | tf_op jit(solution)/shard_map/pallas_call | solution.py:292
  83.9 0.8 copy.15
  84.6 0.8 copy.16
  85.4 0.8 copy.17
  86.2 0.8 copy.18
Async XLA Ops:
  0.6 0.9 %copy-start.4 = (s32[32768]{0:T(1024)S(1)}, s32[32768]{0:T(1024)}, u32[]{:S(2)}) copy-start(s32[32768]{0:T(1024)} %param.10) | copy-start | bytes 393220
  1.6 1.0 %copy-start = (bf16[128,2048]{1,0:T(8,128)(2,1)S(1)}, bf16[128,2048]{1,0:T(8,128)(2,1)}, u32[]{:S(2)}) copy-start(bf16[128,2048]{1,0:T(8,128)(2,1)} %q_ref.1) | copy-start | bytes 1572868
  2.6 1.0 %copy-start.1 = (bf16[128,2048]{1,0:T(8,128)(2,1)S(1)}, bf16[128,2048]{1,0:T(8,128)(2,1)}, u32[]{:S(2)}) copy-start(bf16[128,2048]{1,0:T(8,128)(2,1)} %k_ref.1) | copy-start | bytes 1572868
  3.6 1.0 %copy-start.2 = (bf16[128,2048]{1,0:T(8,128)(2,1)S(1)}, bf16[128,2048]{1,0:T(8,128)(2,1)}, u32[]{:S(2)}) copy-start(bf16[128,2048]{1,0:T(8,128)(2,1)} %v_ref.1) | copy-start | bytes 1572868
  4.7 1.0 %copy-start.3 = (bf16[128,2048]{1,0:T(8,128)(2,1)S(1)}, bf16[128,2048]{1,0:T(8,128)(2,1)}, u32[]{:S(2)}) copy-start(bf16[128,2048]{1,0:T(8,128)(2,1)} %g_ref.1) | copy-start | bytes 1572868

commit v2 on v1

v2 whole, which is shorter than its diff:
```python
import functools
import math

import jax
import jax.numpy as jnp
from jax import lax
from jax.experimental import pallas as pl
from jax.experimental.pallas import tpu as pltpu
from jax.sharding import PartitionSpec as P

HEAD = 128
TILE = 128
HEADS = 16
HALF = 8
PER = 2
GROUPS = HALF // PER
WIDE = PER * HEAD
BLOCKS = 4
MOST = 12
GRAIN = 16
GRAINS = TILE // GRAIN
PLANS = (8, 10, 11, 12)
PIECE = {8: 8, 10: 4, 11: 3, 12: 2}
SCALE = 1.0 / math.sqrt(HEAD)
LOG2E = math.log2(math.e)
FAR = -1e30
MESH_ID = pl.DeviceIdType.MESH


def dot_nt(a, b):
    return lax.dot_general(a, b, (((1,), (1,)), ((), ())), preferred_element_type=jnp.float32)


def dot_nn(a, b):
    return lax.dot_general(a, b, (((1,), (0,)), ((), ())), preferred_element_type=jnp.float32)


def dot_tn(a, b):
    return lax.dot_general(a, b, (((0,), (0,)), ((), ())), preferred_element_type=jnp.float32)


def columns(start, size):
    return pl.ds(pl.multiple_of(start, HEAD), size)


def head_cols(h):
    return slice(h * HEAD, (h + 1) * HEAD)


def grain_rows(start, count):
    return slice(start * GRAIN, (start + count) * GRAIN)


def piece_grain(d, plan, t):
    return GRAINS - PIECE[plan] + t if d == 0 else t


def piece_place(plan, h, t):
    place = h * PIECE[plan] + t
    first = 8 if plan == 8 else plan
    return first + place // GRAINS, place % GRAINS


def relay_source(d, plan, slot, grain):
    first = 8 if plan == 8 else plan
    if slot < first:
        return None
    place = (slot - first) * GRAINS + grain
    h, t = place // PIECE[plan], place % PIECE[plan]
    return (h, piece_grain(d, plan, t)) if h < plan else None


def relay_target(d, plan, h, grain):
    if h >= plan:
        return None
    t = grain - piece_grain(d, plan, 0)
    return piece_place(plan, h, t) if 0 <= t < PIECE[plan] else None


def result_place(plan, h, grain):
    if h >= 12:
        return (h - 12, grain)
    if plan == 8 and grain < 4:
        return (h - 8, grain + 4)
    if plan == 10 and h >= 10 and grain < 5:
        return (2 * (h - 10) + grain // 3, 5 + grain % 3)
    if plan == 11 and h == 11 and grain < 6:
        return (grain // 2, 6 + grain % 2)
    return None


def result_source(plan, block, grain):
    for h in range(8, 12):
        for g in range(GRAINS):
            if result_place(plan, h, g) == (block, grain):
                return (h, g)
    return None


def mirrored(d, grain):
    return grain if d == 0 else GRAINS - 1 - grain


def mirrored_pair(d, pair):
    return None if pair is None else (pair[0], mirrored(d, pair[1]))


def runs(entries):
    start = 0
    for at in range(1, GRAINS + 1):
        joined = at < GRAINS and all(
            (a is None and b is None) or (a is not None and b is not None and a[0] == b[0] and b[1] == a[1] + 1)
            for a, b in zip(entries[at - 1], entries[at])
        )
        if not joined:
            yield start, at - start, entries[start]
            start = at


def kernel(
    n_dp, n_ctx,
    q_ref, k_ref, v_ref, g_ref, ids_hbm, pairs_hbm,
    done,
    own, near, stage, far, result, pack, late, bias, ids_ref, pairs_ref,
    own_sem, side_sem, e1_send, e1_recv, e2_send, e2_recv, late_send, late_recv,
):
    n = n_dp * n_ctx
    me = lax.axis_index("dp") * n_ctx + lax.axis_index("ctx")
    right = lax.rem(me + 1, n)
    left = lax.rem(me + n - 1, n)
    target = [(x // n_ctx, lax.rem(x, n_ctx)) for x in (right, left)]
    inputs = (q_ref, k_ref, v_ref, g_ref)

    def own_copy(a):
        return pltpu.make_async_copy(inputs[a], own.at[a], own_sem.at[a])

    side_copies = [
        pltpu.make_async_copy(ids_hbm, ids_ref, side_sem.at[0]),
        pltpu.make_async_copy(pairs_hbm, pairs_ref, side_sem.at[1]),
    ]

    def first(d, g):
        cols = columns(g * WIDE, WIDE)
        return pltpu.make_async_remote_copy(
            src_ref=own.at[:, :, cols], dst_ref=near.at[d, :, :, cols],
            send_sem=e1_send.at[d, g], recv_sem=e1_recv.at[d, g],
            device_id=target[d], device_id_type=MESH_ID,
        )

    def second(d, s):
        return pltpu.make_async_remote_copy(
            src_ref=stage.at[d, :, :, columns(s * HEAD, HEAD)],
            dst_ref=near.at[d, :, :, columns((HALF + s) * HEAD, HEAD)],
            send_sem=e2_send.at[d, s], recv_sem=e2_recv.at[d, s],
            device_id=target[d], device_id_type=MESH_ID,
        )

    def third(d, j):
        cols = columns(j * HEAD, HEAD)
        return pltpu.make_async_remote_copy(
            src_ref=pack.at[d, :, :, cols], dst_ref=late.at[d, :, :, cols],
            send_sem=late_send.at[d, j], recv_sem=late_recv.at[d, j],
            device_id=target[d], device_id_type=MESH_ID,
        )

    barrier = pltpu.get_barrier_semaphore()
    for d in range(2):
        pl.semaphore_signal(barrier, inc=1, device_id=target[d], device_id_type=MESH_ID)
    for copy in side_copies:
        copy.start()
    for a in range(4):
        own_copy(a).start()
    pl.semaphore_wait(barrier, 2)
    for a in range(4):
        own_copy(a).wait()
    for g in range(GROUPS):
        for d in range(2):
            first(d, g).start()

    for copy in side_copies:
        copy.wait()
    tiles = [lax.rem(me + n + t, n) for t in range(-2, 3)]
    rows = [ids_ref[pl.ds(t, 1), :].astype(jnp.float32) for t in tiles]
    eye = lax.broadcasted_iota(jnp.int32, (TILE, TILE), 0) == lax.broadcasted_iota(jnp.int32, (TILE, TILE), 1)

    def upright(row):
        return jnp.sum(jnp.where(eye, jnp.broadcast_to(row, (TILE, TILE)), 0.0), axis=1, keepdims=True)

    def middle(t):
        before = rows[t - 1][:, TILE - 1 :]
        head, tail = rows[t][:, :1], rows[t][:, TILE - 1 :]
        after = rows[t + 1][:, :1]
        return (before == head) & (head == tail) & (tail == after)

    def plans_of(middle_tile, far_tile):
        count = jnp.sum(jnp.where(rows[far_tile] == rows[middle_tile][:, :1], 1.0, 0.0), axis=1, keepdims=True)
        return {12: count < 33, 11: (count > 32) & (count < 49), 10: (count > 48) & (count < 65), 8: count > 64}

    mid_left, mid_own, mid_right = middle(1), middle(2), middle(3)
    send_plan = [{p: c & mid_own for p, c in plans_of(2, f).items()} for f in (1, 3)]
    recv_plan = [plans_of(1, 0), plans_of(3, 4)]
    codes = pairs_ref[0:1, :] * n + pairs_ref[1:2, :]

    def is_listed(x, y):
        hit = (codes == tiles[x] * n + tiles[y]) | (codes == tiles[y] * n + tiles[x])
        return jnp.max(jnp.where(hit, 1.0, 0.0), axis=1, keepdims=True) > 0.5

    up = [upright(r) for r in rows]
    flags = {}
    for x in range(5):
        for y in range(x, min(x + 3, 5)):
            flags[x, y] = is_listed(x, y)
            flags[y, x] = flags[x, y]
    for x, y in flags:
        seen = (up[x] == rows[y]) & flags[x, y]
        bias[x * TILE : (x + 1) * TILE, y * TILE : (y + 1) * TILE] = jnp.where(seen, 0.0, FAR)
    returned = [
        jnp.where((up[2] == rows[1][:, TILE - 1 :]) & mid_left, 1.0, 0.0),
        jnp.where((up[2] == rows[3][:, :1]) & mid_right, 1.0, 0.0),
    ]


    def pass_on(slot):
        for d in range(2):
            entries = [
                [(slot, grain)] + [relay_source(d, plan, slot, grain) for plan in PLANS] for grain in range(GRAINS)
            ]
            for start, count, sources in runs(entries):
                value = own[:, grain_rows(start, count), head_cols(slot)]
                for plan, source in zip(PLANS, sources[1:]):
                    if source is not None:
                        other = near[d, :, grain_rows(source[1], count), head_cols(source[0])]
                        value = jnp.where(send_plan[d][plan], other, value)
                stage[d, :, grain_rows(start, count), head_cols(slot - HALF)] = value
            second(d, slot - HALF).start()

    def gather_far(h):
        for d in range(2):
            entries = [
                [relay_target(d, plan, h, grain) or (None if plan != 8 else (8, grain)) for plan in PLANS]
                for grain in range(GRAINS)
            ]
            for start, count, sources in runs(entries):
                value = None
                for plan, source in zip(PLANS, sources):
                    if source is not None:
                        other = near[d, :, grain_rows(source[1], count), head_cols(source[0])]
                        value = other if value is None else jnp.where(recv_plan[d][plan], other, value)
                far[d, :, grain_rows(start, count), head_cols(h)] = value

    def softmax_parts(query, grads, keys, values, mask):
        scores = dot_nt(query, keys) * (SCALE * LOG2E) + mask
        top = jnp.max(scores, axis=1, keepdims=True)
        weights = jnp.exp2(scores - top)
        inverse = 1.0 / jnp.sum(weights, axis=1, keepdims=True)
        dprobs = dot_nt(grads, values)
        delta = jnp.sum(weights * dprobs, axis=1, keepdims=True) * inverse
        return weights, inverse, dprobs, delta

    def three_tiles(h):
        at = columns(h * HEAD, HEAD)
        back = columns((h - HALF) * HEAD, HEAD)
        q, k, v, g = [
            jnp.concatenate([near[0, a, :, at], own[a, :, at], near[1, a, :, at]], axis=0) for a in range(4)
        ]
        probs, dscores = [], []

        def put(x, a, value):
            if x == 1:
                done[a, :, at] = value.astype(jnp.bfloat16)
            else:
                result[1 if x == 0 else 0, a, :, back] = value.astype(jnp.bfloat16)

        for x in range(3):
            r = slice(x * TILE, (x + 1) * TILE)
            mask = bias[(x + 1) * TILE : (x + 2) * TILE, TILE : 4 * TILE]
            weights, inverse, dprobs, delta = softmax_parts(q[r], g[r], k, v, mask)
            p = weights * inverse
            p_low = p.astype(jnp.bfloat16)
            ds = (p * (dprobs - delta)).astype(jnp.bfloat16)
            put(x, 0, dot_nn(p_low, v))
            put(x, 1, dot_nn(ds, k) * SCALE)
            probs.append(p_low)
            dscores.append(ds)
        grad_k = dot_tn(jnp.concatenate(dscores, axis=0), q) * SCALE
        grad_v = dot_tn(jnp.concatenate(probs, axis=0), g)
        for x in range(3):
            r = slice(x * TILE, (x + 1) * TILE)
            put(x, 2, grad_k[r])
            put(x, 3, grad_v[r])

    def five_tiles(h):
        at = columns(h * HEAD, HEAD)
        q, k, v, g = [
            jnp.concatenate(
                [far[0, a, :, at], near[0, a, :, at], own[a, :, at], near[1, a, :, at], far[1, a, :, at]], axis=0
            )
            for a in range(4)
        ]
        probs, dscores = [], []
        for x, lo, hi in ((0, 0, 3), (1, 0, 4), (2, 0, 5), (3, 1, 5), (4, 2, 5)):
            r = slice(x * TILE, (x + 1) * TILE)
            c = slice(lo * TILE, hi * TILE)
            weights, inverse, dprobs, delta = softmax_parts(q[r], g[r], k[c], v[c], bias[r, c])
            mine = slice((2 - lo) * TILE, (3 - lo) * TILE)
            if x == 2:
                p = weights * inverse
                p_low = p.astype(jnp.bfloat16)
                ds = (p * (dprobs - delta)).astype(jnp.bfloat16)
                done[0, :, at] = dot_nn(p_low, v).astype(jnp.bfloat16)
                done[1, :, at] = (dot_nn(ds, k) * SCALE).astype(jnp.bfloat16)
                probs.append(p_low[:, mine])
                dscores.append(ds[:, mine])
            else:
                p = weights[:, mine] * inverse
                probs.append(p.astype(jnp.bfloat16))
                dscores.append((p * (dprobs[:, mine] - delta)).astype(jnp.bfloat16))
        done[2, :, at] = (dot_tn(jnp.concatenate(dscores, axis=0), q) * SCALE).astype(jnp.bfloat16)
        done[3, :, at] = dot_tn(jnp.concatenate(probs, axis=0), g).astype(jnp.bfloat16)

    def send_back(j):
        for d in range(2):
            entries = [
                [(12 + j, grain)]
                + [mirrored_pair(d, result_source(plan, j, mirrored(d, grain))) for plan in PLANS]
                for grain in range(GRAINS)
            ]
            for start, count, sources in runs(entries):
                value = result[d, :, grain_rows(start, count), head_cols(4 + j)]
                for plan, source in zip(PLANS, sources[1:]):
                    if source is not None:
                        other = result[d, :, grain_rows(source[1], count), head_cols(source[0] - HALF)]
                        value = jnp.where(send_plan[d][plan], other, value)
                pack[d, :, grain_rows(start, count), head_cols(j)] = value
            third(d, j).start()

    def take_back(h):
        for d in range(2):
            entries = [
                [mirrored_pair(d, result_place(plan, h, mirrored(d, grain))) for plan in PLANS]
                for grain in range(GRAINS)
            ]
            for start, count, sources in runs(entries):
                r = grain_rows(start, count)
                for plan, source in zip(PLANS, sources):
                    if source is None or (h >= 12 and plan != 8):
                        continue
                    take = returned[d][r] > 0.5
                    if h < 12:
                        take = take & recv_plan[d][plan]
                    for a in range(4):
                        other = late[d, a, grain_rows(source[1], count), head_cols(source[0])]
                        done[a, r, head_cols(h)] = jnp.where(take, other, done[a, r, head_cols(h)])

    early_slots = ((8, 9), (10, 11), (12,), (13,))
    for g in range(GROUPS):
        for d in range(2):
            first(d, g).wait_recv()
        for slot in early_slots[g]:
            pass_on(slot)

    ready = ((0, 1, 2, 3), (4, 5), (6, 8, 9, 11), (7, 10))

    def work(h, carry):
        for d in range(2):
            second(d, h - HALF).wait_recv()

        @pl.when(h == 11)
        def _():
            pass_on(14)
            pass_on(15)

        three_tiles(h)
        for j in range(BLOCKS):

            @pl.when(h == 12 + j)
            def _():
                send_back(j)
                for other in ready[j]:
                    gather_far(other)

        @pl.when(h >= 12)
        def _():
            lax.fori_loop(0, 2, lambda i, c: (five_tiles(2 * (h - 12) + i), c)[1], 0)

        return carry

    lax.fori_loop(HALF, HEADS, work, 0)
    lax.fori_loop(HALF, MOST, lambda h, c: (five_tiles(h), c)[1], 0)

    for j in range(BLOCKS):
        for d in range(2):
            third(d, j).wait_recv()
        take_back(12 + j)
        take_back(8 + j)

    for d in range(2):
        for g in range(GROUPS):
            first(d, g).wait_send()
        for s in range(HALF):
            second(d, s).wait_send()
        for j in range(BLOCKS):
            third(d, j).wait_send()


def write_out(done, att_ref, gq_ref, gk_ref, gv_ref, out_sem):
    copies = [
        pltpu.make_async_copy(done.at[a], ref, out_sem.at[a])
        for a, ref in enumerate((att_ref, gq_ref, gk_ref, gv_ref))
    ]
    for copy in copies:
        copy.start()
    for copy in copies:
        copy.wait()


def solution(mesh):
    n_dp, n_ctx = mesh.shape["dp"], mesh.shape["ctx"]
    token_spec = P(("dp", "ctx"), None)

    def body(queries, keys, values, grad_out, doc_ids, tile_pairs):
        width = queries.shape[1]
        in_hbm = pl.BlockSpec(memory_space=pltpu.HBM)
        low = jnp.bfloat16
        sem = pltpu.SemaphoreType.DMA
        held = [
            pltpu.with_memory_space_constraint(x, pltpu.HBM)
            for x in (queries, keys, values, grad_out, doc_ids.reshape(-1, TILE), tile_pairs.T)
        ]
        done = pl.pallas_call(
            functools.partial(kernel, n_dp, n_ctx),
            out_shape=jax.ShapeDtypeStruct((4, TILE, width), low),
            in_specs=[in_hbm] * 6,
            out_specs=pl.BlockSpec(memory_space=pltpu.VMEM),
            scratch_shapes=[
                pltpu.VMEM((4, TILE, width), low),
                pltpu.VMEM((2, 4, TILE, width), low),
                pltpu.VMEM((2, 4, TILE, HALF * HEAD), low),
                pltpu.VMEM((2, 4, TILE, MOST * HEAD), low),
                pltpu.VMEM((2, 4, TILE, HALF * HEAD), low),
                pltpu.VMEM((2, 4, TILE, BLOCKS * HEAD), low),
                pltpu.VMEM((2, 4, TILE, BLOCKS * HEAD), low),
                pltpu.VMEM((5 * TILE, 5 * TILE), jnp.float32),
                pltpu.VMEM((doc_ids.shape[0] // TILE, TILE), jnp.int32),
                pltpu.VMEM((2, tile_pairs.shape[0]), jnp.int32),
                sem((4,)),
                sem((2,)),
                sem((2, GROUPS)),
                sem((2, GROUPS)),
                sem((2, HALF)),
                sem((2, HALF)),
                sem((2, BLOCKS)),
                sem((2, BLOCKS)),
            ],
            compiler_params=pltpu.CompilerParams(
                collective_id=0, has_side_effects=True, vmem_limit_bytes=48 * 1024 * 1024
            ),
        )(*held)
        shape = jax.ShapeDtypeStruct(queries.shape, low)
        return pl.pallas_call(
            write_out,
            out_shape=(shape,) * 4,
            in_specs=[pl.BlockSpec(memory_space=pl.ANY)],
            out_specs=(in_hbm,) * 4,
            scratch_shapes=[sem((4,))],
            compiler_params=pltpu.CompilerParams(vmem_limit_bytes=1024 * 1024),
        )(done)

    return jax.shard_map(
        body,
        mesh=mesh,
        in_specs=(token_spec,) * 4 + (P(), P()),
        out_specs=(token_spec,) * 4,
        check_vma=False,
    )
```

time: 87.3 us -> 74.8 us (0.86)
  local copies, waits for them, and re-layouts: 8.24 us -> 0 us
  Pallas kernels: 78.1 us -> 74.1 us
    unnamed x15 -> x0, local copies, waits for them, and re-layouts: 8.24 us -> none
    pallas_call x1 -> x2, Pallas kernels: 78.1 us -> 74.1 us  [the longest x1 72.7 us: body(): pl.pallas_call(functools.partial(kernel, n_dp, n_ctx), out_shape=jax.Shap...]
where the time goes in v2:
time: 74.8 us; the launch traced here: 74.7 us
  Pallas kernels  74.1 us (99%)
    pallas_call x1, Pallas kernels, body(): pl.pallas_call(functools.partial(kernel, n_dp, n_ctx), out_shape=jax.Shap...  72.7 us

profile of v2, /device:TPU:0, one launch (start us, length us, event | category | flops | bytes accessed | tf_op | source)
XLA Modules:
  0.0 74.7 jit_solution(17585376240658387144)
XLA Ops:
  0.6 72.7 %shard_map.93.done = bf16[4,128,2048]{2,1,0:T(8,128)(2,1)S(1)} custom-call(bf16[128,2048]{1,0:T(8,128)(2,1)} %q_ref.1, bf16[128,2048]{1,0:T(8,128)(2,1)} %k_ref.1, bf16[128,2048]{1,0:T(8,128)(2,1)} %v_ref.1, bf16[128,2048]{1,0:T(8,128)(2,1)} %g_ref.1, s32[256,128]{1,0:T(8,128)} %bitcast.2, s32[2,768]{1,0:T(2,128)} %bitcast.3), custom_call_target="tpu_custom_call" | custom-call | tf_op jit(solution)/shard_map/pallas_call | solution.py:430
  73.4 1.3 %shard_map.94 = (bf16[128,2048]{1,0:T(8,128)(2,1)}, bf16[128,2048]{1,0:T(8,128)(2,1)}, bf16[128,2048]{1,0:T(8,128)(2,1)}, bf16[128,2048]{1,0:T(8,128)(2,1)}) custom-call(bf16[4,128,2048]{2,1,0:T(8,128)(2,1)S(1)} %shard_map.93.done), custom_call_target="tpu_custom_call" | custom-call | tf_op jit(solution)/shard_map/pallas_call | solution.py:460

commit v3 on v2

--- a/solution.py
+++ b/solution.py
@@ -21,6 +21,7 @@
 GRAINS = TILE // GRAIN
 PLANS = (8, 10, 11, 12)
 PIECE = {8: 8, 10: 4, 11: 3, 12: 2}
+ORDER = {8: (12, 11, 10, 9, 8, 13, 14, 15), 10: (12, 11, 10, 13, 14), 11: (12, 11, 13, 14, 15), 12: (12, 13, 14)}
 SCALE = 1.0 / math.sqrt(HEAD)
 LOG2E = math.log2(math.e)
 FAR = -1e30
@@ -57,15 +58,13 @@
 
 def piece_place(plan, h, t):
     place = h * PIECE[plan] + t
-    first = 8 if plan == 8 else plan
-    return first + place // GRAINS, place % GRAINS
+    return ORDER[plan][place // GRAINS], place % GRAINS
 
 
 def relay_source(d, plan, slot, grain):
-    first = 8 if plan == 8 else plan
-    if slot < first:
+    if slot not in ORDER[plan]:
         return None
-    place = (slot - first) * GRAINS + grain
+    place = ORDER[plan].index(slot) * GRAINS + grain
     h, t = place // PIECE[plan], place % PIECE[plan]
     return (h, piece_grain(d, plan, t)) if h < plan else None
 
@@ -121,7 +120,7 @@
     n_dp, n_ctx,
     q_ref, k_ref, v_ref, g_ref, ids_hbm, pairs_hbm,
     done,
-    own, near, stage, far, result, pack, late, bias, ids_ref, pairs_ref,
+    own, near, stage, far, result, pack, late, mask_wide, mask_left, mask_right, from_right, row_kind, ids_ref, pairs_ref,
     own_sem, side_sem, e1_send, e1_recv, e2_send, e2_recv, late_send, late_recv,
 ):
     n = n_dp * n_ctx
@@ -203,7 +202,7 @@
 
     def is_listed(x, y):
         hit = (codes == tiles[x] * n + tiles[y]) | (codes == tiles[y] * n + tiles[x])
-        return jnp.max(jnp.where(hit, 1.0, 0.0), axis=1, keepdims=True) > 0.5
+        return jnp.max(jnp.where(hit, 1.0, 0.0), axis=1, keepdims=True)
 
     up = [upright(r) for r in rows]
     flags = {}
@@ -211,14 +210,62 @@
         for y in range(x, min(x + 3, 5)):
             flags[x, y] = is_listed(x, y)
             flags[y, x] = flags[x, y]
-    for x, y in flags:
-        seen = (up[x] == rows[y]) & flags[x, y]
-        bias[x * TILE : (x + 1) * TILE, y * TILE : (y + 1) * TILE] = jnp.where(seen, 0.0, FAR)
-    returned = [
-        jnp.where((up[2] == rows[1][:, TILE - 1 :]) & mid_left, 1.0, 0.0),
-        jnp.where((up[2] == rows[3][:, :1]) & mid_right, 1.0, 0.0),
-    ]
-
+
+    def number(condition):
+        return jnp.where(condition, 1.0, 0.0)
+
+    def plain(x):
+        return rows[x], up[x], [(x, None, None)]
+
+    def mixed(x, y, along, across):
+        return (
+            jnp.where(along > 0.5, rows[x], rows[y]),
+            jnp.where(across > 0.5, up[x], up[y]),
+            [(x, along, across), (y, 1.0 - along, 1.0 - across)],
+        )
+
+    def mask_of(query_tile, key_tile, keep=None):
+        listed = jnp.zeros((TILE, TILE), jnp.float32)
+        for x, _, across in query_tile[2]:
+            for y, along, _ in key_tile[2]:
+                if (x, y) in flags:
+                    share = jnp.broadcast_to(flags[x, y], (TILE, TILE))
+                    share = share if across is None else share * across
+                    listed += share if along is None else share * along
+        if keep is not None:
+            listed = listed * keep
+        return jnp.where((query_tile[1] == key_tile[0]) & (listed > 0.5), 0.0, FAR)
+
+    far_left = [number((r[0] == rows[1][:, :1]) & mid_left) for r in (rows, up)]
+    far_right = [number((r[4] == rows[3][:, :1]) & mid_right) for r in (rows, up)]
+    take_right = [number((r[1] != rows[2][:, :1]) & mid_own) for r in (rows, up)]
+    far_rows = (far_left[1], far_right[1])
+    centre = plain(2)
+    after = plain(3)
+    near_side = mixed(3, 1, *take_right)
+    left_side = mixed(0, 2, *far_left)
+    right_side = mixed(4, 2, *far_right)
+    one, two, three = slice(0, TILE), slice(TILE, 2 * TILE), slice(2 * TILE, 3 * TILE)
+    not_middle = 1.0 - number(mid_own)
+    mask_wide[one, one] = mask_of(near_side, near_side)
+    mask_wide[one, two] = mask_of(near_side, centre)
+    mask_wide[two, one] = mask_of(centre, near_side)
+    mask_wide[two, two] = mask_of(centre, centre)
+    mask_wide[two, three] = mask_of(centre, after, not_middle)
+    mask_wide[three, two] = mask_of(after, centre, not_middle)
+    mask_wide[three, three] = mask_of(after, after)
+    for ref, x, y in ((mask_left, left_side, near_side), (mask_right, right_side, after)):
+        ref[one, one] = mask_of(x, x)
+        ref[one, two] = mask_of(x, y)
+        ref[two, one] = mask_of(y, x)
+        ref[two, two] = mask_of(y, y)
+    square = (TILE, TILE)
+    from_right[...] = jnp.broadcast_to(take_right[1], square).astype(jnp.bfloat16)
+    reaches_left = number(up[2] == rows[1][:, TILE - 1 :])
+    reaches_right = number(up[2] == rows[3][:, :1])
+    row_kind[0] = jnp.broadcast_to(reaches_left, square)
+    row_kind[1] = jnp.broadcast_to(reaches_right, square)
+    returned = [reaches_left * number(mid_left), reaches_right * number(mid_right)]
 
     def pass_on(slot):
         for d in range(2):
@@ -246,7 +293,9 @@
                     if source is not None:
                         other = near[d, :, grain_rows(source[1], count), head_cols(source[0])]
                         value = other if value is None else jnp.where(recv_plan[d][plan], other, value)
-                far[d, :, grain_rows(start, count), head_cols(h)] = value
+                r = grain_rows(start, count)
+                for a in range(4):
+                    far[d, a, r, head_cols(h)] = jnp.where(far_rows[d][r] > 0.5, value[a], own[a, r, head_cols(h)])
 
     def softmax_parts(query, grads, keys, values, mask):
         scores = dot_nt(query, keys) * (SCALE * LOG2E) + mask
@@ -257,66 +306,75 @@
         delta = jnp.sum(weights * dprobs, axis=1, keepdims=True) * inverse
         return weights, inverse, dprobs, delta
 
+    def load(h):
+        at = columns(h * HEAD, HEAD)
+        after_rows = [near[1, a, :, at] for a in range(4)]
+        use_right = from_right[...] > 0.5
+        near_rows = [jnp.where(use_right, after_rows[a], near[0, a, :, at]) for a in range(4)]
+        return at, near_rows, [own[a, :, at] for a in range(4)], after_rows
+
+    def stacked(*parts):
+        return [jnp.concatenate(part, axis=0) for part in zip(*parts)]
+
+    def full(parts):
+        weights, inverse, dprobs, delta = parts
+        p = weights * inverse
+        return p.astype(jnp.bfloat16), (p * (dprobs - delta)).astype(jnp.bfloat16)
+
+    def partial(parts, cols):
+        weights, inverse, dprobs, delta = parts
+        p = weights[:, cols] * inverse
+        return p.astype(jnp.bfloat16), (p * (dprobs[:, cols] - delta)).astype(jnp.bfloat16)
+
     def three_tiles(h):
-        at = columns(h * HEAD, HEAD)
+        at, near_rows, own_rows, after_rows = load(h)
         back = columns((h - HALF) * HEAD, HEAD)
-        q, k, v, g = [
-            jnp.concatenate([near[0, a, :, at], own[a, :, at], near[1, a, :, at]], axis=0) for a in range(4)
-        ]
-        probs, dscores = [], []
-
-        def put(x, a, value):
-            if x == 1:
-                done[a, :, at] = value.astype(jnp.bfloat16)
-            else:
-                result[1 if x == 0 else 0, a, :, back] = value.astype(jnp.bfloat16)
-
-        for x in range(3):
-            r = slice(x * TILE, (x + 1) * TILE)
-            mask = bias[(x + 1) * TILE : (x + 2) * TILE, TILE : 4 * TILE]
-            weights, inverse, dprobs, delta = softmax_parts(q[r], g[r], k, v, mask)
-            p = weights * inverse
-            p_low = p.astype(jnp.bfloat16)
-            ds = (p * (dprobs - delta)).astype(jnp.bfloat16)
-            put(x, 0, dot_nn(p_low, v))
-            put(x, 1, dot_nn(ds, k) * SCALE)
-            probs.append(p_low)
-            dscores.append(ds)
-        grad_k = dot_tn(jnp.concatenate(dscores, axis=0), q) * SCALE
-        grad_v = dot_tn(jnp.concatenate(probs, axis=0), g)
-        for x in range(3):
-            r = slice(x * TILE, (x + 1) * TILE)
-            put(x, 2, grad_k[r])
-            put(x, 3, grad_v[r])
+        q, k, v, g = stacked(near_rows, own_rows, after_rows)
+        wide = slice(0, 2 * TILE)
+        p_near, ds_near = full(softmax_parts(q[one], g[one], k[wide], v[wide], mask_wide[one, wide]))
+        p_own, ds_own = full(softmax_parts(q[two], g[two], k, v, mask_wide[two, :]))
+        tail = slice(TILE, 3 * TILE)
+        p_after, ds_after = partial(softmax_parts(q[three], g[three], k[tail], v[tail], mask_wide[three, tail]), one)
+        result[0, :, back] = dot_nn(p_near, v[wide]).astype(jnp.bfloat16)
+        result[1, :, back] = (dot_nn(ds_near, k[wide]) * SCALE).astype(jnp.bfloat16)
+        result[2, :, back] = (
+            dot_tn(jnp.concatenate([ds_near[:, one], ds_own[:, one]], axis=0), q[wide]) * SCALE
+        ).astype(jnp.bfloat16)
+        result[3, :, back] = dot_tn(
+            jnp.concatenate([p_near[:, one], p_own[:, one]], axis=0), g[wide]
+        ).astype(jnp.bfloat16)
+        done[0, :, at] = dot_nn(p_own, v).astype(jnp.bfloat16)
+        done[1, :, at] = (dot_nn(ds_own, k) * SCALE).astype(jnp.bfloat16)
+        done[2, :, at] = (
+            dot_tn(jnp.concatenate([ds_near[:, two], ds_own[:, two], ds_after], axis=0), q) * SCALE
+        ).astype(jnp.bfloat16)
+        done[3, :, at] = dot_tn(
+            jnp.concatenate([p_near[:, two], p_own[:, two], p_after], axis=0), g
+        ).astype(jnp.bfloat16)
+
+    def two_tiles(first_rows, second_rows, mask):
+        q, k, v, g = stacked(first_rows, second_rows)
+        p_one, ds_one = full(softmax_parts(q[one], g[one], k, v, mask[one, :]))
+        p_two, ds_two = partial(softmax_parts(q[two], g[two], k, v, mask[two, :]), one)
+        return (
+            dot_nn(p_one, v),
+            dot_nn(ds_one, k) * SCALE,
+            dot_tn(jnp.concatenate([ds_one[:, one], ds_two], axis=0), q) * SCALE,
+            dot_tn(jnp.concatenate([p_one[:, one], p_two], axis=0), g),
+        )
 
     def five_tiles(h):
-        at = columns(h * HEAD, HEAD)
-        q, k, v, g = [
-            jnp.concatenate(
-                [far[0, a, :, at], near[0, a, :, at], own[a, :, at], near[1, a, :, at], far[1, a, :, at]], axis=0
-            )
-            for a in range(4)
-        ]
-        probs, dscores = [], []
-        for x, lo, hi in ((0, 0, 3), (1, 0, 4), (2, 0, 5), (3, 1, 5), (4, 2, 5)):
-            r = slice(x * TILE, (x + 1) * TILE)
-            c = slice(lo * TILE, hi * TILE)
-            weights, inverse, dprobs, delta = softmax_parts(q[r], g[r], k[c], v[c], bias[r, c])
-            mine = slice((2 - lo) * TILE, (3 - lo) * TILE)
-            if x == 2:
-                p = weights * inverse
-                p_low = p.astype(jnp.bfloat16)
-                ds = (p * (dprobs - delta)).astype(jnp.bfloat16)
-                done[0, :, at] = dot_nn(p_low, v).astype(jnp.bfloat16)
-                done[1, :, at] = (dot_nn(ds, k) * SCALE).astype(jnp.bfloat16)
-                probs.append(p_low[:, mine])
-                dscores.append(ds[:, mine])
-            else:
-                p = weights[:, mine] * inverse
-                probs.append(p.astype(jnp.bfloat16))
-                dscores.append((p * (dprobs[:, mine] - delta)).astype(jnp.bfloat16))
-        done[2, :, at] = (dot_tn(jnp.concatenate(dscores, axis=0), q) * SCALE).astype(jnp.bfloat16)
-        done[3, :, at] = dot_tn(jnp.concatenate(probs, axis=0), g).astype(jnp.bfloat16)
+        at, near_rows, own_rows, after_rows = load(h)
+        far_sides = [[far[d, a, :, at] for a in range(4)] for d in range(2)]
+        before = two_tiles(far_sides[0], near_rows, mask_left)
+        behind = two_tiles(far_sides[1], after_rows, mask_right)
+        q, k, v, g = own_rows
+        p, ds = full(softmax_parts(q, g, k, v, mask_wide[two, two]))
+        inside = (dot_nn(p, v), dot_nn(ds, k) * SCALE, dot_tn(ds, q) * SCALE, dot_tn(p, g))
+        on_left, on_right = row_kind[0] > 0.5, row_kind[1] > 0.5
+        for a in range(4):
+            value = jnp.where(on_left, before[a], jnp.where(on_right, behind[a], inside[a]))
+            done[a, :, at] = value.astype(jnp.bfloat16)
 
     def send_back(j):
         for d in range(2):
@@ -326,10 +384,10 @@
                 for grain in range(GRAINS)
             ]
             for start, count, sources in runs(entries):
-                value = result[d, :, grain_rows(start, count), head_cols(4 + j)]
+                value = result[:, grain_rows(start, count), head_cols(4 + j)]
                 for plan, source in zip(PLANS, sources[1:]):
                     if source is not None:
-                        other = result[d, :, grain_rows(source[1], count), head_cols(source[0] - HALF)]
+                        other = result[:, grain_rows(source[1], count), head_cols(source[0] - HALF)]
                         value = jnp.where(send_plan[d][plan], other, value)
                 pack[d, :, grain_rows(start, count), head_cols(j)] = value
             third(d, j).start()
@@ -352,41 +410,42 @@
                         other = late[d, a, grain_rows(source[1], count), head_cols(source[0])]
                         done[a, r, head_cols(h)] = jnp.where(take, other, done[a, r, head_cols(h)])
 
-    early_slots = ((8, 9), (10, 11), (12,), (13,))
+    early_slots = ((), (12,), (11, 10, 9, 8), (13,))
     for g in range(GROUPS):
         for d in range(2):
             first(d, g).wait_recv()
         for slot in early_slots[g]:
             pass_on(slot)
 
-    ready = ((0, 1, 2, 3), (4, 5), (6, 8, 9, 11), (7, 10))
-
-    def work(h, carry):
+    complete = {4: 0, 5: 1, 6: 2, 7: 3}
+    ready = {0: (0,), 1: (1,), 2: (2,), 3: (3,), 5: (4, 5), 6: (6, 8, 9, 11), 7: (7, 10)}
+
+    def work(p, carry):
+        h = jnp.where(p < 5, 12 - p, 8 + p)
         for d in range(2):
             second(d, h - HALF).wait_recv()
 
-        @pl.when(h == 11)
+        @pl.when(p == 4)
         def _():
             pass_on(14)
             pass_on(15)
 
         three_tiles(h)
-        for j in range(BLOCKS):
-
-            @pl.when(h == 12 + j)
+        for step in range(HALF):
+
+            @pl.when(p == step)
             def _():
-                send_back(j)
-                for other in ready[j]:
+                if step in complete:
+                    send_back(complete[step])
+                for other in ready.get(step, ()):
                     gather_far(other)
 
-        @pl.when(h >= 12)
-        def _():
-            lax.fori_loop(0, 2, lambda i, c: (five_tiles(2 * (h - 12) + i), c)[1], 0)
-
+        begin = jnp.where(p == 5, 4, p)
+        end = jnp.where(p == 4, 4, jnp.where(p == 7, MOST, p + 1))
+        lax.fori_loop(begin, end, lambda i, c: (five_tiles(i), c)[1], 0)
         return carry
 
-    lax.fori_loop(HALF, HEADS, work, 0)
-    lax.fori_loop(HALF, MOST, lambda h, c: (five_tiles(h), c)[1], 0)
+    lax.fori_loop(0, HALF, work, 0)
 
     for j in range(BLOCKS):
         for d in range(2):
@@ -437,10 +496,14 @@
                 pltpu.VMEM((2, 4, TILE, width), low),
                 pltpu.VMEM((2, 4, TILE, HALF * HEAD), low),
                 pltpu.VMEM((2, 4, TILE, MOST * HEAD), low),
-                pltpu.VMEM((2, 4, TILE, HALF * HEAD), low),
+                pltpu.VMEM((4, TILE, HALF * HEAD), low),
                 pltpu.VMEM((2, 4, TILE, BLOCKS * HEAD), low),
                 pltpu.VMEM((2, 4, TILE, BLOCKS * HEAD), low),
-                pltpu.VMEM((5 * TILE, 5 * TILE), jnp.float32),
+                pltpu.VMEM((3 * TILE, 3 * TILE), jnp.float32),
+                pltpu.VMEM((2 * TILE, 2 * TILE), jnp.float32),
+                pltpu.VMEM((2 * TILE, 2 * TILE), jnp.float32),
+                pltpu.VMEM((TILE, TILE), low),
+                pltpu.VMEM((2, TILE, TILE), jnp.float32),
                 pltpu.VMEM((doc_ids.shape[0] // TILE, TILE), jnp.int32),
                 pltpu.VMEM((2, tile_pairs.shape[0]), jnp.int32),
                 sem((4,)),

time: 74.8 us -> 71.9 us (0.961)
  Pallas kernels: 74.1 us -> 71.1 us
    pallas_call x1, Pallas kernels: 72.7 us -> 69.8 us  [body(): pl.pallas_call(functools.partial(kernel, n_dp, n_ctx), out_shape=jax.Shap...]
where the time goes in v3:
time: 71.9 us; the launch traced here: 71.8 us
  Pallas kernels  71.1 us (99%)
    pallas_call x1, Pallas kernels, body(): pl.pallas_call(functools.partial(kernel, n_dp, n_ctx), out_shape=jax.Shap...  69.8 us

profile of v3, /device:TPU:0, one launch (start us, length us, event | category | flops | bytes accessed | tf_op | source)
XLA Modules:
  0.0 71.8 jit_solution(6936391148574001753)
XLA Ops:
  0.6 69.8 %shard_map.93.done = bf16[4,128,2048]{2,1,0:T(8,128)(2,1)S(1)} custom-call(bf16[128,2048]{1,0:T(8,128)(2,1)} %q_ref.1, bf16[128,2048]{1,0:T(8,128)(2,1)} %k_ref.1, bf16[128,2048]{1,0:T(8,128)(2,1)} %v_ref.1, bf16[128,2048]{1,0:T(8,128)(2,1)} %g_ref.1, s32[256,128]{1,0:T(8,128)} %bitcast.2, s32[2,768]{1,0:T(2,128)} %bitcast.3), custom_call_target="tpu_custom_call" | custom-call | tf_op jit(solution)/shard_map/pallas_call | solution.py:489
  70.4 1.3 %shard_map.94 = (bf16[128,2048]{1,0:T(8,128)(2,1)}, bf16[128,2048]{1,0:T(8,128)(2,1)}, bf16[128,2048]{1,0:T(8,128)(2,1)}, bf16[128,2048]{1,0:T(8,128)(2,1)}) custom-call(bf16[4,128,2048]{2,1,0:T(8,128)(2,1)S(1)} %shard_map.93.done), custom_call_target="tpu_custom_call" | custom-call | tf_op jit(solution)/shard_map/pallas_call | solution.py:523

commit v4 on v3

--- a/solution.py
+++ b/solution.py
@@ -363,14 +363,17 @@
             dot_tn(jnp.concatenate([p_one[:, one], p_two], axis=0), g),
         )
 
-    def five_tiles(h):
+    def five_tiles(h, known=False):
         at, near_rows, own_rows, after_rows = load(h)
         far_sides = [[far[d, a, :, at] for a in range(4)] for d in range(2)]
         before = two_tiles(far_sides[0], near_rows, mask_left)
         behind = two_tiles(far_sides[1], after_rows, mask_right)
-        q, k, v, g = own_rows
-        p, ds = full(softmax_parts(q, g, k, v, mask_wide[two, two]))
-        inside = (dot_nn(p, v), dot_nn(ds, k) * SCALE, dot_tn(ds, q) * SCALE, dot_tn(p, g))
+        if known:
+            inside = [done[a, :, at].astype(jnp.float32) for a in range(4)]
+        else:
+            q, k, v, g = own_rows
+            p, ds = full(softmax_parts(q, g, k, v, mask_wide[two, two]))
+            inside = (dot_nn(p, v), dot_nn(ds, k) * SCALE, dot_tn(ds, q) * SCALE, dot_tn(p, g))
         on_left, on_right = row_kind[0] > 0.5, row_kind[1] > 0.5
         for a in range(4):
             value = jnp.where(on_left, before[a], jnp.where(on_right, behind[a], inside[a]))
@@ -441,11 +444,12 @@
                     gather_far(other)
 
         begin = jnp.where(p == 5, 4, p)
-        end = jnp.where(p == 4, 4, jnp.where(p == 7, MOST, p + 1))
+        end = jnp.where(p == 4, 4, p + 1)
         lax.fori_loop(begin, end, lambda i, c: (five_tiles(i), c)[1], 0)
         return carry
 
     lax.fori_loop(0, HALF, work, 0)
+    lax.fori_loop(HALF, MOST, lambda h, c: (five_tiles(h, True), c)[1], 0)
 
     for j in range(BLOCKS):
         for d in range(2):

time: 71.9 us -> 71.2 us (level)
  no operation moved by 1% of the time
where the time goes in v4:
time: 71.2 us; the launch traced here: 71.1 us
  Pallas kernels  70.4 us (99%)
    pallas_call x1, Pallas kernels, body(): pl.pallas_call(functools.partial(kernel, n_dp, n_ctx), out_shape=jax.Shap...  69.1 us

profile of v4, /device:TPU:0, one launch (start us, length us, event | category | flops | bytes accessed | tf_op | source)
XLA Modules:
  0.0 71.1 jit_solution(5376731218448295996)
XLA Ops:
  0.6 69.1 %shard_map.93.done = bf16[4,128,2048]{2,1,0:T(8,128)(2,1)S(1)} custom-call(bf16[128,2048]{1,0:T(8,128)(2,1)} %q_ref.1, bf16[128,2048]{1,0:T(8,128)(2,1)} %k_ref.1, bf16[128,2048]{1,0:T(8,128)(2,1)} %v_ref.1, bf16[128,2048]{1,0:T(8,128)(2,1)} %g_ref.1, s32[256,128]{1,0:T(8,128)} %bitcast.2, s32[2,768]{1,0:T(2,128)} %bitcast.3), custom_call_target="tpu_custom_call" | custom-call | tf_op jit(solution)/shard_map/pallas_call | solution.py:493
  69.7 1.3 %shard_map.94 = (bf16[128,2048]{1,0:T(8,128)(2,1)}, bf16[128,2048]{1,0:T(8,128)(2,1)}, bf16[128,2048]{1,0:T(8,128)(2,1)}, bf16[128,2048]{1,0:T(8,128)(2,1)}) custom-call(bf16[4,128,2048]{2,1,0:T(8,128)(2,1)S(1)} %shard_map.93.done), custom_call_target="tpu_custom_call" | custom-call | tf_op jit(solution)/shard_map/pallas_call | solution.py:527

commit v5 on v4

--- a/solution.py
+++ b/solution.py
@@ -21,7 +21,7 @@
 GRAINS = TILE // GRAIN
 PLANS = (8, 10, 11, 12)
 PIECE = {8: 8, 10: 4, 11: 3, 12: 2}
-ORDER = {8: (12, 11, 10, 9, 8, 13, 14, 15), 10: (12, 11, 10, 13, 14), 11: (12, 11, 13, 14, 15), 12: (12, 13, 14)}
+ORDER = {8: (12, 11, 10, 9, 8, 13, 14, 15), 10: (12, 11, 10, 13, 15), 11: (12, 11, 13, 15, 14), 12: (12, 13, 15)}
 SCALE = 1.0 / math.sqrt(HEAD)
 LOG2E = math.log2(math.e)
 FAR = -1e30
@@ -421,16 +421,19 @@
             pass_on(slot)
 
     complete = {4: 0, 5: 1, 6: 2, 7: 3}
-    ready = {0: (0,), 1: (1,), 2: (2,), 3: (3,), 5: (4, 5), 6: (6, 8, 9, 11), 7: (7, 10)}
+    ready = {0: (0,), 1: (1,), 2: (2,), 3: (3,), 5: (4, 5), 6: (6,), 7: (7, 8, 9, 10, 11)}
 
     def work(p, carry):
         h = jnp.where(p < 5, 12 - p, 8 + p)
         for d in range(2):
             second(d, h - HALF).wait_recv()
 
+        @pl.when(p == 2)
+        def _():
+            pass_on(14)
+
         @pl.when(p == 4)
         def _():
-            pass_on(14)
             pass_on(15)
 
         three_tiles(h)

time: 71.2 us -> 70.5 us (level)
  no operation moved by 1% of the time
where the time goes in v5:
time: 70.5 us; the launch traced here: 70.4 us
  Pallas kernels  69.8 us (99%)
    pallas_call x1, Pallas kernels, body(): pl.pallas_call(functools.partial(kernel, n_dp, n_ctx), out_shape=jax.Shap...  68.5 us

profile of v5, /device:TPU:0, one launch (start us, length us, event | category | flops | bytes accessed | tf_op | source)
XLA Modules:
  0.0 70.4 jit_solution(14652856139737812712)
XLA Ops:
  0.6 68.5 %shard_map.93.done = bf16[4,128,2048]{2,1,0:T(8,128)(2,1)S(1)} custom-call(bf16[128,2048]{1,0:T(8,128)(2,1)} %q_ref.1, bf16[128,2048]{1,0:T(8,128)(2,1)} %k_ref.1, bf16[128,2048]{1,0:T(8,128)(2,1)} %v_ref.1, bf16[128,2048]{1,0:T(8,128)(2,1)} %g_ref.1, s32[256,128]{1,0:T(8,128)} %bitcast.2, s32[2,768]{1,0:T(2,128)} %bitcast.3), custom_call_target="tpu_custom_call" | custom-call | tf_op jit(solution)/shard_map/pallas_call | solution.py:496
  69.1 1.3 %shard_map.94 = (bf16[128,2048]{1,0:T(8,128)(2,1)}, bf16[128,2048]{1,0:T(8,128)(2,1)}, bf16[128,2048]{1,0:T(8,128)(2,1)}, bf16[128,2048]{1,0:T(8,128)(2,1)}) custom-call(bf16[4,128,2048]{2,1,0:T(8,128)(2,1)S(1)} %shard_map.93.done), custom_call_target="tpu_custom_call" | custom-call | tf_op jit(solution)/shard_map/pallas_call | solution.py:530

commit v6 on v5

--- a/solution.py
+++ b/solution.py
@@ -470,8 +470,10 @@
 
 
 def write_out(done, att_ref, gq_ref, gk_ref, gv_ref, out_sem):
+    half = TILE // 2
     copies = [
-        pltpu.make_async_copy(done.at[a], ref, out_sem.at[a])
+        pltpu.make_async_copy(done.at[a, pl.ds(b * half, half)], ref.at[pl.ds(b * half, half)], out_sem.at[a, b])
+        for b in range(2)
         for a, ref in enumerate((att_ref, gq_ref, gk_ref, gv_ref))
     ]
     for copy in copies:
@@ -532,7 +534,7 @@
             out_shape=(shape,) * 4,
             in_specs=[pl.BlockSpec(memory_space=pl.ANY)],
             out_specs=(in_hbm,) * 4,
-            scratch_shapes=[sem((4,))],
+            scratch_shapes=[sem((4, 2))],
             compiler_params=pltpu.CompilerParams(vmem_limit_bytes=1024 * 1024),
         )(done)
 

time: 70.5 us -> 70.6 us (level)
  no operation moved by 1% of the time
where the time goes in v6:
time: 70.6 us; the launch traced here: 70.5 us
  Pallas kernels  69.8 us (99%)
    pallas_call x1, Pallas kernels, body(): pl.pallas_call(functools.partial(kernel, n_dp, n_ctx), out_shape=jax.Shap...  68.5 us

profile of v6, /device:TPU:0, one launch (start us, length us, event | category | flops | bytes accessed | tf_op | source)
XLA Modules:
  0.0 70.5 jit_solution(15076543601498754434)
XLA Ops:
  0.6 68.5 %shard_map.93.done = bf16[4,128,2048]{2,1,0:T(8,128)(2,1)S(1)} custom-call(bf16[128,2048]{1,0:T(8,128)(2,1)} %q_ref.1, bf16[128,2048]{1,0:T(8,128)(2,1)} %k_ref.1, bf16[128,2048]{1,0:T(8,128)(2,1)} %v_ref.1, bf16[128,2048]{1,0:T(8,128)(2,1)} %g_ref.1, s32[256,128]{1,0:T(8,128)} %bitcast.2, s32[2,768]{1,0:T(2,128)} %bitcast.3), custom_call_target="tpu_custom_call" | custom-call | tf_op jit(solution)/shard_map/pallas_call | solution.py:498
  69.1 1.4 %shard_map.94 = (bf16[128,2048]{1,0:T(8,128)(2,1)}, bf16[128,2048]{1,0:T(8,128)(2,1)}, bf16[128,2048]{1,0:T(8,128)(2,1)}, bf16[128,2048]{1,0:T(8,128)(2,1)}) custom-call(bf16[4,128,2048]{2,1,0:T(8,128)(2,1)S(1)} %shard_map.93.done), custom_call_target="tpu_custom_call" | custom-call | tf_op jit(solution)/shard_map/pallas_call | solution.py:532
